TPU v7x, 32 devices: a whole 2x2x4 slice. The times are simulated.
32 devices in a mesh: grp: 2 (over x), blk: 16 (over z, y, core).
Axes of the slice: x: 2, y: 2, z: 4, core: 2. Of those that a mesh axis runs over, the one named last changes fastest.
Arguments:
- position: float32 [1536, 64, 128], P(('grp', 'blk')), parts along dimension 0, may hold values from -3 to 3
- momentum: float32 [1536, 64, 128], P(('grp', 'blk')), parts along dimension 0, may hold values from -6 to 6
- counts: int32 [1536, 64, 128], P(('grp', 'blk')), parts along dimension 0, may hold values from 0 to 5
- neighbours: int32 [768, 4], P('blk'), may hold values from -1 to 766, as said below
- cond_factor: bfloat16 [768, 4, 128, 128], P('blk'), may hold values from -0.25 to 0.25
- whiten: bfloat16 [768, 128, 128], P('blk')
Outputs:
- position_end: float32 [1536, 64, 128], P(('grp', 'blk')), parts along dimension 0
- momentum_end: float32 [1536, 64, 128], P(('grp', 'blk')), parts along dimension 0
- energy_change: float32 [128], P('grp'), parts along dimension 0
There are 2 independent parts, one for each index of `grp`. A program takes and returns all parts, laid end to end along the dimension named above; an argument that names none is the same for every part. Nothing has to cross between parts.
Inputs may be any that keep to these rules, and one draw needn't show every extreme that they name: `neighbours`: row b lists block b - 1 first, then three other distinct blocks from b - 96 to b - 2; an entry is -1 exactly where that block would fall before block 0.
All inputs are finite; a program needn't handle non-finite values.
Results may differ from a plain program's by a relative error of at most 0.0018.
Values may be sent and summed in bfloat16 or wider, within the bound.
A program may use at most 128 MiB of HBM per device.

v0:
```python
import jax
import jax.numpy as jnp
from jax import lax
from jax.sharding import PartitionSpec as P

leap_size = 0.3


def passed_along(value, axis, steps):
    count = lax.axis_size(axis)
    leading, last = (max(0, -steps), min(count, count - steps))
    return lax.ppermute(value, axis, [(source, source + steps) for source in range(leading, last)])


def per_device(position, momentum, counts, neighbours, cond_factor, whiten):
    blocks = position.shape[0]
    chains = position.shape[1]
    points = position.shape[2]
    first_block = (lax.axis_index("blk") - 2) * blocks
    present = neighbours >= 0
    window_index = jnp.clip(neighbours - first_block, 0, 3 * blocks - 1)
    present_half = present.astype(jnp.bfloat16)[:, :, None, None]
    present_full = present.astype(jnp.float32)[:, :, None, None]
    target_slot = jnp.where(present, window_index, 3 * blocks).reshape(-1)
    weight = counts.astype(jnp.float32)

    def gradient(field):
        rounded = field.astype(jnp.bfloat16)
        earlier = passed_along(rounded, "blk", 1)
        farther = passed_along(rounded, "blk", 2)
        window = jnp.concatenate([farther, earlier, rounded], axis=0)
        nearby = window[window_index] * present_half
        cond_mean = jnp.einsum(
            "bkij,bkcj->bci", cond_factor, nearby, preferred_element_type=jnp.float32
        )
        innovation = (field - cond_mean).astype(jnp.bfloat16)
        whitened = jnp.einsum(
            "bij,bcj->bci", whiten, innovation, preferred_element_type=jnp.float32
        )
        pulled = jnp.einsum(
            "bij,bci->bcj",
            whiten,
            whitened.astype(jnp.bfloat16),
            preferred_element_type=jnp.float32,
        )
        pushed = -jnp.einsum(
            "bkij,bci->bkcj",
            cond_factor,
            pulled.astype(jnp.bfloat16),
            preferred_element_type=jnp.float32,
        )
        pushed = pushed * present_full
        gathered = (
            jnp.zeros((3 * blocks, chains, points), jnp.float32)
            .at[target_slot]
            .add(pushed.reshape(4 * blocks, chains, points), mode="drop")
        )
        far_terms = gathered[:blocks]
        near_terms = gathered[blocks : 2 * blocks]
        own_terms = gathered[2 * blocks :]
        returned = (
            own_terms + passed_along(near_terms, "blk", -1) + passed_along(far_terms, "blk", -2)
        )
        grad = pulled + returned + jnp.exp(field) - weight
        cell = 0.5 * whitened * whitened + jnp.exp(field) - weight * field
        return (grad, cell)

    grad, cell_start = gradient(position)
    moment = momentum - 0.5 * leap_size * grad
    field = position + leap_size * moment
    grad, cell = gradient(field)
    moment = moment - leap_size * grad
    field = field + leap_size * moment
    grad, cell_end = gradient(field)
    moment = moment - 0.5 * leap_size * grad
    change = cell_end + 0.5 * moment * moment - cell_start - 0.5 * momentum * momentum
    total = lax.psum(jnp.sum(change, axis=(0, 2)), "blk")
    return (field, moment, total)


def solution(mesh):
    return jax.shard_map(
        per_device,
        mesh=mesh,
        in_specs=(
            P(("grp", "blk"), None, None),
            P(("grp", "blk"), None, None),
            P(("grp", "blk"), None, None),
            P("blk", None),
            P("blk", None, None, None),
            P("blk", None, None),
        ),
        out_specs=(P(("grp", "blk"), None, None), P(("grp", "blk"), None, None), P("grp")),
        check_vma=False,
    )
```

profile of v0, /device:TPU:0, one launch (start us, length us, event | category | flops | bytes accessed | tf_op | source)
XLA Modules:
  0.0 469.5 jit_solution(6311475270701455686)
XLA Ops:
  4.7 5.3 %collective-permute-start = (bf16[48,64,128]{2,1,0:T(8,128)(2,1)S(1)}, bf16[48,64,128]{2,1,0:T(8,128)(2,1)}, u32[]{:S(2)}, u32[]{:S(2)}) collective-permute-start(bf16[48,64,128]{2,1,0:T(8,128)(2,1)S(1)} %convert_element_type.45), channel_id=1, source_target_pairs={{0,2},{1,3},{2,4},{3,5},{4,6},{5,7},{6,8},{7,9},{8,10},{9,11},{10,... | collective-permute-start | bytes 2359304 | tf_op jit(solution)/shard_map/ppermute | solution.py:12
  10.7 16.4 %collective-permute-done = bf16[48,64,128]{2,1,0:T(8,128)(2,1)} collective-permute-done((bf16[48,64,128]{2,1,0:T(8,128)(2,1)S(1)}, bf16[48,64,128]{2,1,0:T(8,128)(2,1)}, u32[]{:S(2)}, u32[]{:S(2)}) %collective-permute-start) | collective-permute-done | bytes 786464 | tf_op jit(solution)/shard_map/ppermute | solution.py:12
  30.0 4.5 gather_fusion
  34.5 8.3 %fusion.41 = f32[48,64,128]{2,1,0:T(8,128)} fusion(bf16[48,128,128]{2,1,0:T(8,128)(2,1)S(1)} %copy-done, f32[48,64,128]{2,1,0:T(8,128)S(1)} %copy-done.1, bf16[48,4,128,128]{3,2,1,0:T(8,128)(2,1)} %param.10, bf16[48,4,64,128]{3,2,1,0:T(8,128)(2,1)} %bitcast.64, bf16[48,4]{1,0:T(8,128)(2,1)S(1)} %copy.12), kind=kOutput, calls=%fused_computation.63 | convolution fusion | flops 505675776 | bytes 14156160 | tf_op jit(solution)/shard_map/bij,bcj->bci/dot_general | solution.py:37
  44.7 7.0 %negate_multiply_fusion.2 = f32[48,64,4,128]{3,1,2,0:T(8,128)} fusion(f32[48,4]{1,0:T(8,128)S(1)} %copy.14, bf16[48,4,128,128]{3,2,1,0:T(8,128)(2,1)} %param.10, f32[48,64,128]{2,1,0:T(8,128)S(1)} %fusion.59), kind=kOutput, calls=%fused_computation.8 | convolution fusion | flops 406192128 | bytes 14156544 | tf_op jit(solution)/shard_map/bkij,bci->bkcj/dot_general | solution.py:46
  54.5 31.9 %scatter_fusion = f32[144,64,128]{2,1,0:T(8,128)} fusion(f32[144,64,128]{2,1,0:T(8,128)} %broadcast.42.clone, s32[192]{0:T(256)S(1)} %bitcast.66, f32[192,64,128]{2,1,0:T(8,128)} %bitcast.61), kind=kCustom, calls=%fused_computation.3 | custom fusion | flops 1572864 | bytes 18875136 | tf_op jit(solution)/shard_map/scatter-add | solution.py:56
  91.4 32.5 %collective-permute-done.3 = f32[48,64,128]{2,1,0:T(8,128)S(1)} collective-permute-done((f32[48,64,128]{2,1,0:T(8,128)S(1)}, f32[48,64,128]{2,1,0:T(8,128)S(1)}, u32[]{:S(2)}, u32[]{:S(2)}) %collective-permute-start.3) | collective-permute-done | bytes 1572896 | tf_op jit(solution)/shard_map/ppermute | solution.py:12
  127.8 22.6 %collective-permute-start.5 = (bf16[48,64,128]{2,1,0:T(8,128)(2,1)S(1)}, bf16[48,64,128]{2,1,0:T(8,128)(2,1)S(1)}, u32[]{:S(2)}, u32[]{:S(2)}) collective-permute-start(bf16[48,64,128]{2,1,0:T(8,128)(2,1)S(1)} %get-tuple-element.8), channel_id=1, source_target_pairs={{0,1},{1,2},{2,3},{3,4},{4,5},{5,6},{6,7},{7,8},{8,9},{9,10},{10,1... | collective-permute-start | bytes 2359304 | tf_op jit(solution)/shard_map/ppermute | solution.py:12
  154.5 17.7 %collective-permute-done.4 = bf16[48,64,128]{2,1,0:T(8,128)(2,1)S(1)} collective-permute-done((bf16[48,64,128]{2,1,0:T(8,128)(2,1)S(1)}, bf16[48,64,128]{2,1,0:T(8,128)(2,1)S(1)}, u32[]{:S(2)}, u32[]{:S(2)}) %collective-permute-start.4) | collective-permute-done | bytes 786464 | tf_op jit(solution)/shard_map/ppermute | solution.py:12
  173.9 4.4 gather_fusion.1
  178.3 7.3 %fusion.33 = bf16[48,64,128]{2,1,0:T(8,128)(2,1)} fusion(bf16[48,4,128,128]{3,2,1,0:T(8,128)(2,1)} %param.10, bf16[48,4,64,128]{3,2,1,0:T(8,128)(2,1)} %bitcast.65, bf16[48,4]{1,0:T(8,128)(2,1)S(1)} %copy.12, f32[48,64,128]{2,1,0:T(8,128)S(1)} %copy-done.1, f32[48,64,128]{2,1,0:T(8,128)} %get-tuple-element.9), kind=kOutput, calls=%fused_computation.54 | convolution fusion | flops 405798912 | bytes 13369728 | tf_op jit(solution)/shard_map/bkij,bkcj->bci/dot_general | solution.py:33
  189.6 6.9 %negate_multiply_fusion.1 = f32[48,64,4,128]{3,1,2,0:T(8,128)} fusion(f32[48,4]{1,0:T(8,128)S(1)} %copy.14, bf16[48,4,128,128]{3,2,1,0:T(8,128)(2,1)} %param.10, f32[48,64,128]{2,1,0:T(8,128)} %fusion.50), kind=kOutput, calls=%fused_computation.7 | convolution fusion | flops 406192128 | bytes 14156544 | tf_op jit(solution)/shard_map/bkij,bci->bkcj/dot_general | solution.py:46
  199.3 31.9 %scatter_fusion.1 = f32[144,64,128]{2,1,0:T(8,128)} fusion(f32[144,64,128]{2,1,0:T(8,128)} %broadcast.42.clone.1, s32[192]{0:T(256)S(1)} %bitcast.67, f32[192,64,128]{2,1,0:T(8,128)} %bitcast.62), kind=kCustom, calls=%fused_computation.4 | custom fusion | flops 1572864 | bytes 18875136 | tf_op jit(solution)/shard_map/scatter-add | solution.py:56
  236.2 34.6 %collective-permute-done.7 = f32[48,64,128]{2,1,0:T(8,128)S(1)} collective-permute-done((f32[48,64,128]{2,1,0:T(8,128)S(1)}, f32[48,64,128]{2,1,0:T(8,128)S(1)}, u32[]{:S(2)}, u32[]{:S(2)}) %collective-permute-start.7) | collective-permute-done | bytes 1572896 | tf_op jit(solution)/shard_map/ppermute | solution.py:12
  270.8 4.8 %fusion.66 = (bf16[48,64,128]{2,1,0:T(8,128)(2,1)S(1)}, f32[48,64,128]{2,1,0:T(8,128)}, f32[48,64,128]{2,1,0:T(8,128)}) fusion(f32[48,64,128]{2,1,0:T(8,128)S(1)} %copy-done.1, f32[48,64,128]{2,1,0:T(8,128)S(1)} %copy-done.2, s32[48,64,128]{2,1,0:T(8,128)S(1)} %copy-done.7, f32[48,64,128]{2,1,0:T(8,128)S(1)} %copy-done.3, ...), kind=kLoop, calls=%fused_computation.85 | loop fusion | flops 5111808 | bytes 14942208 | tf_op jit(solution)/shard_map/convert_element_type | solution.py:28
  275.6 20.5 %collective-permute-start.9 = (bf16[48,64,128]{2,1,0:T(8,128)(2,1)S(1)}, bf16[48,64,128]{2,1,0:T(8,128)(2,1)S(1)}, u32[]{:S(2)}, u32[]{:S(2)}) collective-permute-start(bf16[48,64,128]{2,1,0:T(8,128)(2,1)S(1)} %get-tuple-element.5), channel_id=1, source_target_pairs={{0,1},{1,2},{2,3},{3,4},{4,5},{5,6},{6,7},{7,8},{8,9},{9,10},{10,1... | collective-permute-start | bytes 2359304 | tf_op jit(solution)/shard_map/ppermute | solution.py:12
  300.1 17.7 %collective-permute-done.8 = bf16[48,64,128]{2,1,0:T(8,128)(2,1)S(1)} collective-permute-done((bf16[48,64,128]{2,1,0:T(8,128)(2,1)S(1)}, bf16[48,64,128]{2,1,0:T(8,128)(2,1)S(1)}, u32[]{:S(2)}, u32[]{:S(2)}) %collective-permute-start.8) | collective-permute-done | bytes 786464 | tf_op jit(solution)/shard_map/ppermute | solution.py:12
  319.5 4.4 gather_fusion.2
  323.9 8.7 %fusion.48 = f32[48,64,128]{2,1,0:T(8,128)} fusion(bf16[48,128,128]{2,1,0:T(8,128)(2,1)S(1)} %copy-done, f32[48,64,128]{2,1,0:T(8,128)} %get-tuple-element.6, bf16[48,4,128,128]{3,2,1,0:T(8,128)(2,1)} %param.10, bf16[48,4,64,128]{3,2,1,0:T(8,128)(2,1)} %bitcast.63, bf16[48,4]{1,0:T(8,128)(2,1)S(1)} %copy.12), kind=kOutput, calls=%fused_computation.64 | convolution fusion | flops 505675776 | bytes 14156160 | tf_op jit(solution)/shard_map/bij,bcj->bci/dot_general | solution.py:37
  334.5 7.0 %negate_multiply_fusion = f32[48,64,4,128]{3,1,2,0:T(8,128)} fusion(f32[48,4]{1,0:T(8,128)S(1)} %copy.14, bf16[48,4,128,128]{3,2,1,0:T(8,128)(2,1)} %param.10, f32[48,64,128]{2,1,0:T(8,128)S(1)} %fusion.55), kind=kOutput, calls=%fused_computation.6 | convolution fusion | flops 406192128 | bytes 14156544 | tf_op jit(solution)/shard_map/bkij,bci->bkcj/dot_general | solution.py:46
  344.3 31.9 %scatter_fusion.2 = f32[144,64,128]{2,1,0:T(8,128)} fusion(f32[144,64,128]{2,1,0:T(8,128)} %broadcast.42, s32[192]{0:T(256)S(1)} %bitcast.68, f32[192,64,128]{2,1,0:T(8,128)} %bitcast.60), kind=kCustom, calls=%fused_computation.5 | custom fusion | flops 1572864 | bytes 18875136 | tf_op jit(solution)/shard_map/scatter-add | solution.py:56
  381.2 34.5 %collective-permute-done.11 = f32[48,64,128]{2,1,0:T(8,128)S(1)} collective-permute-done((f32[48,64,128]{2,1,0:T(8,128)S(1)}, f32[48,64,128]{2,1,0:T(8,128)S(1)}, u32[]{:S(2)}, u32[]{:S(2)}) %collective-permute-start.11) | collective-permute-done | bytes 1572896 | tf_op jit(solution)/shard_map/ppermute | solution.py:12
  415.7 5.1 %fusion.11 = (f32[64]{0:T(128)S(1)}, f32[48,64,128]{2,1,0:T(8,128)}) fusion(f32[48,64,128]{2,1,0:T(8,128)S(1)} %copy-done.11, f32[48,64,128]{2,1,0:T(8,128)S(1)} %copy-done.10, f32[48,64,128]{2,1,0:T(8,128)} %param.7, f32[48,64,128]{2,1,0:T(8,128)S(1)} %copy-done.1, f32[48,64,128]{2,1,0:T(8,128)S(1)} %copy-done.9, s32[48,64,128]{2,1,0:T(8,128)S(1)} %copy-done.8, ...), kind=kLoop, calls=%fused_computation.27 | loop fusion | flops 10223552 | bytes 18874624 | tf_op jit(solution)/shard_map/reduce_sum | solution.py:77
  420.8 48.7 %psum.7 = f32[64]{0:T(128)} all-reduce(f32[64]{0:T(128)S(1)} %get-tuple-element.3), channel_id=1, replica_groups=mesh['grp'=2,'blk'=16] {'blk'}, use_global_device_ids=true, to_apply=%region_4.5 | all-reduce | flops 64 | bytes 512 | tf_op jit(solution)/shard_map/psum | solution.py:77
  (69 shorter events, 54.0 us)
Async XLA Ops:
  0.6 33.8 %copy-start = (bf16[48,128,128]{2,1,0:T(8,128)(2,1)S(1)}, bf16[48,128,128]{2,1,0:T(8,128)(2,1)}, u32[]{:S(2)}) copy-start(bf16[48,128,128]{2,1,0:T(8,128)(2,1)} %param.11) | copy-start | bytes 4718596
  0.6 9.4 %copy-start.14 = (s32[48,4]{0,1:T(4,128)S(1)}, s32[48,4]{0,1:T(4,128)}, u32[]{:S(2)}) copy-start(s32[48,4]{0,1:T(4,128)} %param.9) | copy-start | bytes 2308
  2.3 8.3 %collective-permute-start.1 = (bf16[48,64,128]{2,1,0:T(8,128)(2,1)S(1)}, bf16[48,64,128]{2,1,0:T(8,128)(2,1)S(1)}, u32[]{:S(2)}, u32[]{:S(2)}) collective-permute-start(bf16[48,64,128]{2,1,0:T(8,128)(2,1)S(1)} %convert_element_type.45), channel_id=1, source_target_pairs={{0,1},{1,2},{2,3},{3,4},{4,5},{5,6},{6,7},{7,8},{8,9},{9,10},{10,1... | collective-permute-start | bytes 2359304 | tf_op jit(solution)/shard_map/ppermute | solution.py:12
  4.7 22.4 %collective-permute-start = (bf16[48,64,128]{2,1,0:T(8,128)(2,1)S(1)}, bf16[48,64,128]{2,1,0:T(8,128)(2,1)}, u32[]{:S(2)}, u32[]{:S(2)}) collective-permute-start(bf16[48,64,128]{2,1,0:T(8,128)(2,1)S(1)} %convert_element_type.45), channel_id=1, source_target_pairs={{0,2},{1,3},{2,4},{3,5},{4,6},{5,7},{6,8},{7,9},{8,10},{9,11},{10,... | collective-permute-start | bytes 2359304 | tf_op jit(solution)/shard_map/ppermute | solution.py:12
  86.4 37.5 %copy-start.5 = (f32[48,64,128]{2,1,0:T(8,128)S(1)}, f32[48,64,128]{2,1,0:T(8,128)}, u32[]{:S(2)}) copy-start(f32[48,64,128]{2,1,0:T(8,128)} %copy-done.4) | copy-start | bytes 4718596
  86.4 37.5 %copy-start.6 = (s32[48,64,128]{2,1,0:T(8,128)S(1)}, s32[48,64,128]{2,1,0:T(8,128)}, u32[]{:S(2)}) copy-start(s32[48,64,128]{2,1,0:T(8,128)} %param.8) | copy-start | bytes 4718596
  86.4 37.6 %copy-start.13 = (f32[48,64,128]{2,1,0:T(8,128)S(1)}, f32[48,64,128]{2,1,0:T(8,128)}, u32[]{:S(2)}) copy-start(f32[48,64,128]{2,1,0:T(8,128)} %param.7) | copy-start | bytes 4718596
  88.6 35.3 %collective-permute-start.3 = (f32[48,64,128]{2,1,0:T(8,128)S(1)}, f32[48,64,128]{2,1,0:T(8,128)S(1)}, u32[]{:S(2)}, u32[]{:S(2)}) collective-permute-start(f32[48,64,128]{2,1,0:T(8,128)S(1)} %get-tuple-element.15), channel_id=1, source_target_pairs={{2,0},{3,1},{4,2},{5,3},{6,4},{7,5},{8,6},{9,7},{10,8},{11,9},{12,... | collective-permute-start | bytes 4718600 | tf_op jit(solution)/shard_map/ppermute | solution.py:12
  90.1 33.8 %collective-permute-start.2 = (f32[48,64,128]{2,1,0:T(8,128)S(1)}, f32[48,64,128]{2,1,0:T(8,128)S(1)}, u32[]{:S(2)}, u32[]{:S(2)}) collective-permute-start(f32[48,64,128]{2,1,0:T(8,128)S(1)} %get-tuple-element.14), channel_id=1, source_target_pairs={{1,0},{2,1},{3,2},{4,3},{5,4},{6,5},{7,6},{8,7},{9,8},{10,9},{11,1... | collective-permute-start | bytes 4718600 | tf_op jit(solution)/shard_map/ppermute | solution.py:12
  127.8 26.6 %collective-permute-start.5 = (bf16[48,64,128]{2,1,0:T(8,128)(2,1)S(1)}, bf16[48,64,128]{2,1,0:T(8,128)(2,1)S(1)}, u32[]{:S(2)}, u32[]{:S(2)}) collective-permute-start(bf16[48,64,128]{2,1,0:T(8,128)(2,1)S(1)} %get-tuple-element.8), channel_id=1, source_target_pairs={{0,1},{1,2},{2,3},{3,4},{4,5},{5,6},{6,7},{7,8},{8,9},{9,10},{10,1... | collective-permute-start | bytes 2359304 | tf_op jit(solution)/shard_map/ppermute | solution.py:12
  150.5 21.7 %collective-permute-start.4 = (bf16[48,64,128]{2,1,0:T(8,128)(2,1)S(1)}, bf16[48,64,128]{2,1,0:T(8,128)(2,1)S(1)}, u32[]{:S(2)}, u32[]{:S(2)}) collective-permute-start(bf16[48,64,128]{2,1,0:T(8,128)(2,1)S(1)} %get-tuple-element.8), channel_id=1, source_target_pairs={{0,2},{1,3},{2,4},{3,5},{4,6},{5,7},{6,8},{7,9},{8,10},{9,11},{10,... | collective-permute-start | bytes 2359304 | tf_op jit(solution)/shard_map/ppermute | solution.py:12
  231.2 39.6 %copy-start.2 = (f32[48,64,128]{2,1,0:T(8,128)S(1)}, f32[48,64,128]{2,1,0:T(8,128)}, u32[]{:S(2)}) copy-start(f32[48,64,128]{2,1,0:T(8,128)} %get-tuple-element.9) | copy-start | bytes 4718596
  231.2 39.6 %copy-start.3 = (f32[48,64,128]{2,1,0:T(8,128)S(1)}, f32[48,64,128]{2,1,0:T(8,128)}, u32[]{:S(2)}) copy-start(f32[48,64,128]{2,1,0:T(8,128)} %fusion.50) | copy-start | bytes 4718596
  231.2 39.6 %copy-start.7 = (s32[48,64,128]{2,1,0:T(8,128)S(1)}, s32[48,64,128]{2,1,0:T(8,128)}, u32[]{:S(2)}) copy-start(s32[48,64,128]{2,1,0:T(8,128)} %param.8) | copy-start | bytes 4718596
  233.4 37.4 %collective-permute-start.7 = (f32[48,64,128]{2,1,0:T(8,128)S(1)}, f32[48,64,128]{2,1,0:T(8,128)S(1)}, u32[]{:S(2)}, u32[]{:S(2)}) collective-permute-start(f32[48,64,128]{2,1,0:T(8,128)S(1)} %get-tuple-element.13), channel_id=1, source_target_pairs={{2,0},{3,1},{4,2},{5,3},{6,4},{7,5},{8,6},{9,7},{10,8},{11,9},{12,... | collective-permute-start | bytes 4718600 | tf_op jit(solution)/shard_map/ppermute | solution.py:12
  234.9 35.9 %collective-permute-start.6 = (f32[48,64,128]{2,1,0:T(8,128)S(1)}, f32[48,64,128]{2,1,0:T(8,128)S(1)}, u32[]{:S(2)}, u32[]{:S(2)}) collective-permute-start(f32[48,64,128]{2,1,0:T(8,128)S(1)} %get-tuple-element.12), channel_id=1, source_target_pairs={{1,0},{2,1},{3,2},{4,3},{5,4},{6,5},{7,6},{8,7},{9,8},{10,9},{11,1... | collective-permute-start | bytes 4718600 | tf_op jit(solution)/shard_map/ppermute | solution.py:12
  275.6 24.5 %collective-permute-start.9 = (bf16[48,64,128]{2,1,0:T(8,128)(2,1)S(1)}, bf16[48,64,128]{2,1,0:T(8,128)(2,1)S(1)}, u32[]{:S(2)}, u32[]{:S(2)}) collective-permute-start(bf16[48,64,128]{2,1,0:T(8,128)(2,1)S(1)} %get-tuple-element.5), channel_id=1, source_target_pairs={{0,1},{1,2},{2,3},{3,4},{4,5},{5,6},{6,7},{7,8},{8,9},{9,10},{10,1... | collective-permute-start | bytes 2359304 | tf_op jit(solution)/shard_map/ppermute | solution.py:12
  296.1 21.6 %collective-permute-start.8 = (bf16[48,64,128]{2,1,0:T(8,128)(2,1)S(1)}, bf16[48,64,128]{2,1,0:T(8,128)(2,1)S(1)}, u32[]{:S(2)}, u32[]{:S(2)}) collective-permute-start(bf16[48,64,128]{2,1,0:T(8,128)(2,1)S(1)} %get-tuple-element.5), channel_id=1, source_target_pairs={{0,2},{1,3},{2,4},{3,5},{4,6},{5,7},{6,8},{7,9},{8,10},{9,11},{10,... | collective-permute-start | bytes 2359304 | tf_op jit(solution)/shard_map/ppermute | solution.py:12
  376.2 39.5 %copy-start.8 = (s32[48,64,128]{2,1,0:T(8,128)S(1)}, s32[48,64,128]{2,1,0:T(8,128)}, u32[]{:S(2)}) copy-start(s32[48,64,128]{2,1,0:T(8,128)} %param.8) | copy-start | bytes 4718596
  376.2 39.5 %copy-start.9 = (f32[48,64,128]{2,1,0:T(8,128)S(1)}, f32[48,64,128]{2,1,0:T(8,128)}, u32[]{:S(2)}) copy-start(f32[48,64,128]{2,1,0:T(8,128)} %get-tuple-element.6) | copy-start | bytes 4718596
  376.2 39.5 %copy-start.10 = (f32[48,64,128]{2,1,0:T(8,128)S(1)}, f32[48,64,128]{2,1,0:T(8,128)}, u32[]{:S(2)}) copy-start(f32[48,64,128]{2,1,0:T(8,128)} %fusion.41) | copy-start | bytes 4718596
  376.2 39.5 %copy-start.11 = (f32[48,64,128]{2,1,0:T(8,128)S(1)}, f32[48,64,128]{2,1,0:T(8,128)}, u32[]{:S(2)}) copy-start(f32[48,64,128]{2,1,0:T(8,128)} %fusion.48) | copy-start | bytes 4718596
  378.5 37.2 %collective-permute-start.11 = (f32[48,64,128]{2,1,0:T(8,128)S(1)}, f32[48,64,128]{2,1,0:T(8,128)S(1)}, u32[]{:S(2)}, u32[]{:S(2)}) collective-permute-start(f32[48,64,128]{2,1,0:T(8,128)S(1)} %get-tuple-element.11), channel_id=1, source_target_pairs={{2,0},{3,1},{4,2},{5,3},{6,4},{7,5},{8,6},{9,7},{10,8},{11,9},{12,... | collective-permute-start | bytes 4718600 | tf_op jit(solution)/shard_map/ppermute | solution.py:12
  379.9 35.8 %collective-permute-start.10 = (f32[48,64,128]{2,1,0:T(8,128)S(1)}, f32[48,64,128]{2,1,0:T(8,128)S(1)}, u32[]{:S(2)}, u32[]{:S(2)}) collective-permute-start(f32[48,64,128]{2,1,0:T(8,128)S(1)} %get-tuple-element.10), channel_id=1, source_target_pairs={{1,0},{2,1},{3,2},{4,3},{5,4},{6,5},{7,6},{8,7},{9,8},{10,9},{11,1... | collective-permute-start | bytes 4718600 | tf_op jit(solution)/shard_map/ppermute | solution.py:12
  (3 other events, 18.5 us)
where the time goes:
time: 471 us; the launch traced here: 470 us
  waiting for transfers between devices  154 us (33%)
  other arithmetic  117 us (25%)
  starting transfers between devices  66.9 us (14%)
  matrix products  53 us (11%)
  blocking collectives  48.7 us (10%)
  local copies, waits for them, and re-layouts  29.1 us (6%)
    ppermute x12, waiting for transfers between devices, passed_along(): lax.ppermute(value, axis, [(source, source + steps) for source in range(l...  154 us
    scatter-add x3, other arithmetic, gradient(): gathered = jnp.zeros((3 * blocks, chains, points), jnp.float32).at[target...  95.6 us
    ppermute x12, starting transfers between devices, passed_along(): lax.ppermute(value, axis, [(source, source + steps) for source in range(l...  66.9 us
    psum x1, blocking collectives, per_device(): total = lax.psum(jnp.sum(change, axis=(0, 2)), 'blk')  48.7 us
    dot_general x3, matrix products, gradient(): jnp.einsum('bkij,bci->bkcj', cond_factor, pulled.astype(jnp.bfloat16), pr...  20.9 us
    dot_general x2, matrix products, gradient(): jnp.einsum('bij,bcj->bci', whiten, innovation, preferred_element_type=jnp...  16.9 us
    gather x3, local copies, waits for them, and re-layouts, gradient(): nearby = window[window_index] * present_half  13.3 us
    convert_element_type x3, other arithmetic, gradient(): rounded = field.astype(jnp.bfloat16)  10.3 us
  transfers between devices with their start and end apart: 12, of which 6 were waited for; matrix products, arithmetic and copies ran while one was open for 0% of the time, Pallas kernels for 0%

commit v1 on v0

v1 whole, which is shorter than its diff:
```python
import functools

import jax
import jax.numpy as jnp
from jax import lax
from jax.experimental import pallas as pl
from jax.experimental.pallas import tpu as pltpu
from jax.sharding import PartitionSpec as P

leap_size = 0.3
GROUP = 8


def nt(a, b):
    return lax.dot_general(a, b, (((1,), (1,)), ((), ())), preferred_element_type=jnp.float32)


def nn(a, b):
    return lax.dot_general(a, b, (((1,), (0,)), ((), ())), preferred_element_type=jnp.float32)


def terms_kernel(
    group, slots, far_in, near_in, own_in, field, cond, whiten,
    far_out, near_out, own_out, square_out,
    window, acc, sems,
):
    blocks = far_in.shape[0]
    step = pl.program_id(0)
    steps = pl.num_programs(0)

    @pl.when(step == 0)
    def _():
        copies = [
            pltpu.make_async_copy(part, window.at[pl.ds(at * blocks, blocks)], sems.at[at])
            for at, part in enumerate((far_in, near_in, own_in))
        ]
        for copy in copies:
            copy.start()
        window[3 * blocks] = jnp.zeros(window.shape[1:], window.dtype)
        square_out[...] = jnp.zeros_like(square_out)

        @pl.loop(0, 3 * blocks + 1)
        def _(at):
            acc[at] = jnp.zeros(acc.shape[1:], acc.dtype)

        for copy in copies:
            copy.wait()

    base = step * group
    where = [[slots[(base + g) * 4 + k] for k in range(4)] for g in range(group)]
    innovations = []
    for g in range(group):
        nearby = jnp.concatenate([window[where[g][k]] for k in range(4)], axis=1)
        factor = jnp.concatenate([cond[g, k] for k in range(4)], axis=1)
        innovations.append((field[g] - nt(nearby, factor)).astype(jnp.bfloat16))
    whitened = [nt(innovations[g], whiten[g]) for g in range(group)]
    square = square_out[...]
    for g in range(group):
        square = square + whitened[g] * whitened[g]
    square_out[...] = square
    pulled = [nn(whitened[g].astype(jnp.bfloat16), whiten[g]) for g in range(group)]
    for g in range(group):
        factor = jnp.concatenate([cond[g, k] for k in range(4)], axis=1)
        pushed = nn(pulled[g].astype(jnp.bfloat16), factor)
        points = pulled[g].shape[1]
        for k in range(4):
            acc[where[g][k]] -= pushed[:, k * points : (k + 1) * points]
        acc[2 * blocks + base + g] += pulled[g]

    @pl.when(step == steps - 1)
    def _():
        @pl.loop(0, blocks)
        def _(at):
            far_out[at] = acc[at]
            near_out[at] = acc[blocks + at].astype(near_out.dtype)
            own_out[at] = acc[2 * blocks + at]


def terms(slots, far, near, own, field, cond, whiten):
    blocks, chains, points = field.shape
    group = GROUP if blocks % GROUP == 0 else 1
    whole = pl.BlockSpec((blocks, chains, points), lambda s, i: (0, 0, 0))
    hbm = pl.BlockSpec(memory_space=pl.ANY)
    return pl.pallas_call(
        functools.partial(terms_kernel, group),
        grid_spec=pltpu.PrefetchScalarGridSpec(
            num_scalar_prefetch=1,
            grid=(blocks // group,),
            in_specs=[
                hbm, hbm, hbm,
                pl.BlockSpec((group, chains, points), lambda s, i: (s, 0, 0)),
                pl.BlockSpec((group, 4, points, points), lambda s, i: (s, 0, 0, 0)),
                pl.BlockSpec((group, points, points), lambda s, i: (s, 0, 0)),
            ],
            out_specs=[whole, whole, whole, pl.BlockSpec((chains, points), lambda s, i: (0, 0))],
            scratch_shapes=[
                pltpu.VMEM((3 * blocks + 1, chains, points), jnp.bfloat16),
                pltpu.VMEM((3 * blocks + 1, chains, points), jnp.float32),
                pltpu.SemaphoreType.DMA((3,)),
            ],
        ),
        out_shape=[
            jax.ShapeDtypeStruct(field.shape, jnp.float32),
            jax.ShapeDtypeStruct(field.shape, jnp.bfloat16),
            jax.ShapeDtypeStruct(field.shape, jnp.float32),
            jax.ShapeDtypeStruct((chains, points), jnp.float32),
        ],
        compiler_params=pltpu.CompilerParams(vmem_limit_bytes=40 * 2**20),
        cost_estimate=pl.CostEstimate(
            flops=20 * blocks * chains * points * points, bytes_accessed=20 * 2**20, transcendentals=0
        ),
        name="terms",
    )(slots, far, near, own, field, cond, whiten)


def shifted(value, steps):
    count = lax.axis_size("blk")
    leading, last = (max(0, -steps), min(count, count - steps))
    return lax.ppermute(value, "blk", [(source, source + steps) for source in range(leading, last)])


def swapped(value):
    count = lax.axis_size("blk")
    return lax.ppermute(value, "blk", [(source, source ^ 1) for source in range(count)])


def per_device(position, momentum, counts, neighbours, cond_factor, whiten):
    blocks = position.shape[0]
    me = lax.axis_index("blk")
    odd = lax.rem(me, 2) == 1
    first_block = (me - 2) * blocks
    slots = jnp.where(
        neighbours >= 0, jnp.clip(neighbours - first_block, 0, 3 * blocks - 1), 3 * blocks
    ).reshape(-1)
    weight = counts.astype(jnp.float32)

    def gradient(field):
        rounded = field.astype(jnp.bfloat16)
        farther = shifted(rounded, 2)
        earlier = swapped(jnp.where(odd, farther, rounded))
        far, near, own, square = terms(
            slots, farther, earlier, rounded, field, cond_factor, whiten
        )
        other = swapped(near).astype(jnp.float32)
        back = (far + jnp.where(odd, other, 0.0)).astype(jnp.bfloat16)
        own = own + jnp.where(odd, 0.0, other)
        grad = own + shifted(back, -2).astype(jnp.float32) + jnp.exp(field) - weight
        return grad, square

    def local_cell(field):
        return jnp.exp(field) - weight * field

    grad, square_start = gradient(position)
    moment = momentum - 0.5 * leap_size * grad
    field = position + leap_size * moment
    grad, _ = gradient(field)
    moment = moment - leap_size * grad
    field = field + leap_size * moment
    grad, square_end = gradient(field)
    moment = moment - 0.5 * leap_size * grad
    change = (
        local_cell(field) + 0.5 * moment * moment - local_cell(position) - 0.5 * momentum * momentum
    )
    change = jnp.sum(change, axis=0) + 0.5 * (square_end - square_start)
    total = lax.psum(jnp.sum(change, axis=1), "blk")
    return (field, moment, total)


def solution(mesh):
    return jax.shard_map(
        per_device,
        mesh=mesh,
        in_specs=(
            P(("grp", "blk"), None, None),
            P(("grp", "blk"), None, None),
            P(("grp", "blk"), None, None),
            P("blk", None),
            P("blk", None, None, None),
            P("blk", None, None),
        ),
        out_specs=(P(("grp", "blk"), None, None), P(("grp", "blk"), None, None), P("grp")),
        check_vma=False,
    )
```

time: 471 us -> 220 us (0.47)
  other arithmetic: 117 us -> 9.65 us
  matrix products: 53 us -> 0 us
  starting transfers between devices: 66.9 us -> 19.6 us
  Pallas kernels: 0 us -> 31.4 us
  waiting for transfers between devices: 154 us -> 125 us
  local copies, waits for them, and re-layouts: 29.1 us -> 0.22 us
  blocking collectives: 48.7 us -> 32.6 us
    scatter-add x3 -> x0, other arithmetic: 95.6 us -> none  [gradient(): gathered = jnp.zeros((3 * blocks, chains, points), jnp.float32).at[target...]
    dot_general x9 -> x0, matrix products: 53 us -> none  [the longest x3 20.9 us: gradient(): jnp.einsum('bkij,bci->bkcj', cond_factor, pulled.astype(jnp.bfloat16), pr...]
    ppermute x12, starting transfers between devices: 66.9 us -> 19.6 us  [the longest x6 19 us: shifted(): lax.ppermute(value, 'blk', [(source, source + steps) for source in range(...]
    pallas_call x0 -> x3, Pallas kernels: none -> 31.4 us  [terms(): pl.pallas_call(functools.partial(terms_kernel, group), grid_spec=pltpu.Pr...]
    ppermute x12, waiting for transfers between devices: 154 us -> 125 us  [the longest x6 111 us: shifted(): lax.ppermute(value, 'blk', [(source, source + steps) for source in range(...]
    psum x1, blocking collectives: 48.7 us -> 32.6 us  [per_device(): total = lax.psum(jnp.sum(change, axis=1), 'blk')]
    gather x3 -> x0, local copies, waits for them, and re-layouts: 13.3 us -> none  [gradient(): nearby = window[window_index] * present_half]
    another operation x3 -> x0, local copies, waits for them, and re-layouts: 8.46 us -> none
  transfers between devices with their start and end apart: 12 -> 12, of which waited for: 6 -> 12; matrix products, arithmetic and copies ran while one was open for 0% -> 0% of each run, Pallas kernels for 0% -> 0%
where the time goes in v1:
time: 220 us; the launch traced here: 219 us
  waiting for transfers between devices  125 us (57%)
  blocking collectives  32.6 us (15%)
  Pallas kernels  31.4 us (14%)
  starting transfers between devices  19.6 us (9%)
  other arithmetic  9.65 us (4%)
    ppermute x6, waiting for transfers between devices, shifted(): lax.ppermute(value, 'blk', [(source, source + steps) for source in range(...  111 us
    psum x1, blocking collectives, per_device(): total = lax.psum(jnp.sum(change, axis=1), 'blk')  32.6 us
    pallas_call x3, Pallas kernels, terms(): pl.pallas_call(functools.partial(terms_kernel, group), grid_spec=pltpu.Pr...  31.4 us
    ppermute x6, starting transfers between devices, shifted(): lax.ppermute(value, 'blk', [(source, source + steps) for source in range(...  19 us
    ppermute x6, waiting for transfers between devices, swapped(): lax.ppermute(value, 'blk', [(source, source ^ 1) for source in range(coun...  13.5 us
    convert_element_type x3, other arithmetic, gradient(): rounded = field.astype(jnp.bfloat16)  4.59 us
  transfers between devices with their start and end apart: 12, of which 12 were waited for; matrix products, arithmetic and copies ran while one was open for 0% of the time, Pallas kernels for 0%

profile of v1, /device:TPU:0, one launch (start us, length us, event | category | flops | bytes accessed | tf_op | source)
XLA Modules:
  0.0 219.0 jit_solution(6000818310774762898)
XLA Ops:
  0.6 2.5 %convert_element_type.39.own_in = bf16[48,64,128]{2,1,0:T(8,128)(2,1)} convert(f32[48,64,128]{2,1,0:T(8,128)} %field.1) | non-fusion elementwise | flops 393216 | bytes 2359296 | tf_op jit(solution)/shard_map/convert_element_type | solution.py:138
  3.2 5.8 %collective-permute-start = (bf16[48,64,128]{2,1,0:T(8,128)(2,1)}, bf16[48,64,128]{2,1,0:T(8,128)(2,1)}, u32[]{:S(2)}, u32[]{:S(2)}) collective-permute-start(bf16[48,64,128]{2,1,0:T(8,128)(2,1)} %convert_element_type.39.own_in), channel_id=1, source_target_pairs={{0,2},{1,3},{2,4},{3,5},{4,6},{5,7},{6,8},{7,9},{8,10},{9,11},{10,... | collective-permute-start | bytes 2359304 | tf_op jit(solution)/shard_map/ppermute | solution.py:119
  9.0 16.2 %collective-permute-done.far_in = bf16[48,64,128]{2,1,0:T(8,128)(2,1)} collective-permute-done((bf16[48,64,128]{2,1,0:T(8,128)(2,1)}, bf16[48,64,128]{2,1,0:T(8,128)(2,1)}, u32[]{:S(2)}, u32[]{:S(2)}) %collective-permute-start) | collective-permute-done | bytes 786464 | tf_op jit(solution)/shard_map/ppermute | solution.py:119
  26.4 2.3 %collective-permute-done.1.near_in = bf16[48,64,128]{2,1,0:T(8,128)(2,1)} collective-permute-done((bf16[48,64,128]{2,1,0:T(8,128)(2,1)}, bf16[48,64,128]{2,1,0:T(8,128)(2,1)}, u32[]{:S(2)}, u32[]{:S(2)}) %collective-permute-start.1) | collective-permute-done | bytes 786464 | tf_op jit(solution)/shard_map/ppermute | solution.py:124
  28.8 10.8 %terms.3 = (f32[48,64,128]{2,1,0:T(8,128)S(1)}, bf16[48,64,128]{2,1,0:T(8,128)(2,1)S(1)}, f32[48,64,128]{2,1,0:T(8,128)S(1)}, f32[64,128]{1,0:T(8,128)S(1)}) custom-call(s32[192]{0:T(256)S(1)} %reshape.9.slots, bf16[48,64,128]{2,1,0:T(8,128)(2,1)} %collective-permute-done.far_in, bf16[48,64,128]{2,1,0:T(8,128)(2,1)} %collective-permute-done.1.near_in, ...), custom_call_target="tpu_custom_call" | custom-call | flops 1006632960 | bytes 20971520 | tf_op jit(solution)/shard_map/terms/pallas_call | solution.py:84
  39.7 2.2 %collective-permute-done.2 = bf16[48,64,128]{2,1,0:T(8,128)(2,1)S(1)} collective-permute-done((bf16[48,64,128]{2,1,0:T(8,128)(2,1)S(1)}, bf16[48,64,128]{2,1,0:T(8,128)(2,1)S(1)}, u32[]{:S(2)}, u32[]{:S(2)}) %collective-permute-start.2) | collective-permute-done | bytes 786464 | tf_op jit(solution)/shard_map/ppermute | solution.py:124
  42.2 1.4 collective-permute-start.3
  43.6 20.9 %collective-permute-done.3 = bf16[48,64,128]{2,1,0:T(8,128)(2,1)S(1)} collective-permute-done((bf16[48,64,128]{2,1,0:T(8,128)(2,1)S(1)}, bf16[48,64,128]{2,1,0:T(8,128)(2,1)S(1)}, u32[]{:S(2)}, u32[]{:S(2)}) %collective-permute-start.3) | collective-permute-done | bytes 786464 | tf_op jit(solution)/shard_map/ppermute | solution.py:119
  65.5 4.6 %collective-permute-start.4 = (bf16[48,64,128]{2,1,0:T(8,128)(2,1)S(1)}, bf16[48,64,128]{2,1,0:T(8,128)(2,1)S(1)}, u32[]{:S(2)}, u32[]{:S(2)}) collective-permute-start(bf16[48,64,128]{2,1,0:T(8,128)(2,1)S(1)} %get-tuple-element.29.own_in), channel_id=1, source_target_pairs={{0,2},{1,3},{2,4},{3,5},{4,6},{5,7},{6,8},{7,9},{8,10},{9,11},{10,... | collective-permute-start | bytes 2359304 | tf_op jit(solution)/shard_map/ppermute | solution.py:119
  70.1 16.2 %collective-permute-done.4.far_in = bf16[48,64,128]{2,1,0:T(8,128)(2,1)S(1)} collective-permute-done((bf16[48,64,128]{2,1,0:T(8,128)(2,1)S(1)}, bf16[48,64,128]{2,1,0:T(8,128)(2,1)S(1)}, u32[]{:S(2)}, u32[]{:S(2)}) %collective-permute-start.4) | collective-permute-done | bytes 786464 | tf_op jit(solution)/shard_map/ppermute | solution.py:119
  86.5 2.3 %collective-permute-done.5.near_in = bf16[48,64,128]{2,1,0:T(8,128)(2,1)S(1)} collective-permute-done((bf16[48,64,128]{2,1,0:T(8,128)(2,1)S(1)}, bf16[48,64,128]{2,1,0:T(8,128)(2,1)S(1)}, u32[]{:S(2)}, u32[]{:S(2)}) %collective-permute-start.5) | collective-permute-done | bytes 786464 | tf_op jit(solution)/shard_map/ppermute | solution.py:124
  88.7 10.6 %terms.4 = (f32[48,64,128]{2,1,0:T(8,128)S(1)}, bf16[48,64,128]{2,1,0:T(8,128)(2,1)S(1)}, f32[48,64,128]{2,1,0:T(8,128)S(1)}, f32[64,128]{1,0:T(8,128)}) custom-call(s32[192]{0:T(256)S(1)} %reshape.9.slots, bf16[48,64,128]{2,1,0:T(8,128)(2,1)S(1)} %collective-permute-done.4.far_in, bf16[48,64,128]{2,1,0:T(8,128)(2,1)S(1)} %collective-permute-done.5.near_in, ...), custom_call_target="tpu_custom_call" | custom-call | flops 1006632960 | bytes 20971520 | tf_op jit(solution)/shard_map/terms/pallas_call | solution.py:84
  99.5 2.2 %collective-permute-done.6 = bf16[48,64,128]{2,1,0:T(8,128)(2,1)S(1)} collective-permute-done((bf16[48,64,128]{2,1,0:T(8,128)(2,1)S(1)}, bf16[48,64,128]{2,1,0:T(8,128)(2,1)S(1)}, u32[]{:S(2)}, u32[]{:S(2)}) %collective-permute-start.6) | collective-permute-done | bytes 786464 | tf_op jit(solution)/shard_map/ppermute | solution.py:124
  102.0 1.3 collective-permute-start.7
  103.3 20.9 %collective-permute-done.7 = bf16[48,64,128]{2,1,0:T(8,128)(2,1)S(1)} collective-permute-done((bf16[48,64,128]{2,1,0:T(8,128)(2,1)S(1)}, bf16[48,64,128]{2,1,0:T(8,128)(2,1)S(1)}, u32[]{:S(2)}, u32[]{:S(2)}) %collective-permute-start.7) | collective-permute-done | bytes 786464 | tf_op jit(solution)/shard_map/ppermute | solution.py:119
  125.2 4.6 %collective-permute-start.8 = (bf16[48,64,128]{2,1,0:T(8,128)(2,1)S(1)}, bf16[48,64,128]{2,1,0:T(8,128)(2,1)S(1)}, u32[]{:S(2)}, u32[]{:S(2)}) collective-permute-start(bf16[48,64,128]{2,1,0:T(8,128)(2,1)S(1)} %get-tuple-element.27.own_in), channel_id=1, source_target_pairs={{0,2},{1,3},{2,4},{3,5},{4,6},{5,7},{6,8},{7,9},{8,10},{9,11},{10,... | collective-permute-start | bytes 2359304 | tf_op jit(solution)/shard_map/ppermute | solution.py:119
  129.8 16.2 %collective-permute-done.8.far_in = bf16[48,64,128]{2,1,0:T(8,128)(2,1)S(1)} collective-permute-done((bf16[48,64,128]{2,1,0:T(8,128)(2,1)S(1)}, bf16[48,64,128]{2,1,0:T(8,128)(2,1)S(1)}, u32[]{:S(2)}, u32[]{:S(2)}) %collective-permute-start.8) | collective-permute-done | bytes 786464 | tf_op jit(solution)/shard_map/ppermute | solution.py:119
  146.2 2.3 %collective-permute-done.9.near_in = bf16[48,64,128]{2,1,0:T(8,128)(2,1)S(1)} collective-permute-done((bf16[48,64,128]{2,1,0:T(8,128)(2,1)S(1)}, bf16[48,64,128]{2,1,0:T(8,128)(2,1)S(1)}, u32[]{:S(2)}, u32[]{:S(2)}) %collective-permute-start.9) | collective-permute-done | bytes 786464 | tf_op jit(solution)/shard_map/ppermute | solution.py:124
  148.4 10.0 %terms.5 = (f32[48,64,128]{2,1,0:T(8,128)S(1)}, bf16[48,64,128]{2,1,0:T(8,128)(2,1)S(1)}, f32[48,64,128]{2,1,0:T(8,128)S(1)}, f32[64,128]{1,0:T(8,128)S(1)}) custom-call(s32[192]{0:T(256)S(1)} %reshape.9.slots, bf16[48,64,128]{2,1,0:T(8,128)(2,1)S(1)} %collective-permute-done.8.far_in, bf16[48,64,128]{2,1,0:T(8,128)(2,1)S(1)} %collective-permute-done.9.near_in, ...), custom_call_target="tpu_custom_call" | custom-call | flops 1006632960 | bytes 20971520 | tf_op jit(solution)/shard_map/terms/pallas_call | solution.py:84
  158.6 2.2 %collective-permute-done.10 = bf16[48,64,128]{2,1,0:T(8,128)(2,1)S(1)} collective-permute-done((bf16[48,64,128]{2,1,0:T(8,128)(2,1)S(1)}, bf16[48,64,128]{2,1,0:T(8,128)(2,1)S(1)}, u32[]{:S(2)}, u32[]{:S(2)}) %collective-permute-start.10) | collective-permute-done | bytes 786464 | tf_op jit(solution)/shard_map/ppermute | solution.py:124
  161.1 1.3 collective-permute-start.11
  162.4 20.9 %collective-permute-done.11 = bf16[48,64,128]{2,1,0:T(8,128)(2,1)S(1)} collective-permute-done((bf16[48,64,128]{2,1,0:T(8,128)(2,1)S(1)}, bf16[48,64,128]{2,1,0:T(8,128)(2,1)S(1)}, u32[]{:S(2)}, u32[]{:S(2)}) %collective-permute-start.11) | collective-permute-done | bytes 786464 | tf_op jit(solution)/shard_map/ppermute | solution.py:119
  183.2 3.0 %fusion.27 = (f32[64,128]{1,0:T(8,128)S(1)}, f32[48,64,128]{2,1,0:T(8,128)}) fusion(f32[48,64,128]{2,1,0:T(8,128)S(1)} %copy-done.4, f32[48,64,128]{2,1,0:T(8,128)S(1)} %copy-done, f32[48,64,128]{2,1,0:T(8,128)S(1)} %get-tuple-element.28.field, s32[48,64,128]{2,1,0:T(8,128)S(1)} %copy-done.3, bf16[48,64,128]{2,1,0:T(8,128)(2,1)S(1)} %collective-permute-done.11, ...), kind=kLoop, calls=%fused_computation.35 | loop fusion | flops 12181504 | bytes 17334272 | tf_op jit(solution)/shard_map/reduce_sum | solution.py:164
  186.4 32.6 %psum.7 = f32[64]{0:T(128)} all-reduce(f32[64]{0:T(128)S(1)} %add_reduce_fusion), channel_id=1, replica_groups=mesh['grp'=2,'blk'=16] {'blk'}, use_global_device_ids=true, to_apply=%region_2.3 | all-reduce | flops 64 | bytes 512 | tf_op jit(solution)/shard_map/psum | solution.py:165
  (30 shorter events, 4.9 us)
Async XLA Ops:
  0.6 24.5 %copy-start = (f32[48,64,128]{2,1,0:T(8,128)S(1)}, f32[48,64,128]{2,1,0:T(8,128)}, u32[]{:S(2)}) copy-start(f32[48,64,128]{2,1,0:T(8,128)} %field.1) | copy-start | bytes 4718596
  3.2 22.0 %collective-permute-start = (bf16[48,64,128]{2,1,0:T(8,128)(2,1)}, bf16[48,64,128]{2,1,0:T(8,128)(2,1)}, u32[]{:S(2)}, u32[]{:S(2)}) collective-permute-start(bf16[48,64,128]{2,1,0:T(8,128)(2,1)} %convert_element_type.39.own_in), channel_id=1, source_target_pairs={{0,2},{1,3},{2,4},{3,5},{4,6},{5,7},{6,8},{7,9},{8,10},{9,11},{10,... | collective-permute-start | bytes 2359304 | tf_op jit(solution)/shard_map/ppermute | solution.py:119
  9.0 17.3 %copy-start.5 = (s32[48,4]{0,1:T(4,128)S(1)}, s32[48,4]{0,1:T(4,128)}, u32[]{:S(2)}) copy-start(s32[48,4]{0,1:T(4,128)} %param.9) | copy-start | bytes 2308
  9.0 19.8 %copy-start.1 = (bf16[48,128,128]{2,1,0:T(8,128)(2,1)S(1)}, bf16[48,128,128]{2,1,0:T(8,128)(2,1)}, u32[]{:S(2)}) copy-start(bf16[48,128,128]{2,1,0:T(8,128)(2,1)} %whiten.5) | copy-start | bytes 4718596
  26.1 2.6 %collective-permute-start.1 = (bf16[48,64,128]{2,1,0:T(8,128)(2,1)}, bf16[48,64,128]{2,1,0:T(8,128)(2,1)}, u32[]{:S(2)}, u32[]{:S(2)}) collective-permute-start(bf16[48,64,128]{2,1,0:T(8,128)(2,1)} %broadcast_select_fusion.2), channel_id=1, source_target_pairs={{0,1},{1,0},{2,3},{3,2},{4,5},{5,4},{6,7},{7,6},{8,9},{9,8},{10,11... | collective-permute-start | bytes 2359304 | tf_op jit(solution)/shard_map/ppermute | solution.py:124
  39.6 2.4 %collective-permute-start.2 = (bf16[48,64,128]{2,1,0:T(8,128)(2,1)S(1)}, bf16[48,64,128]{2,1,0:T(8,128)(2,1)S(1)}, u32[]{:S(2)}, u32[]{:S(2)}) collective-permute-start(bf16[48,64,128]{2,1,0:T(8,128)(2,1)S(1)} %get-tuple-element.15), channel_id=1, source_target_pairs={{0,1},{1,0},{2,3},{3,2},{4,5},{5,4},{6,7},{7,6},{8,9},{9,8},{10,11... | collective-permute-start | bytes 2359304 | tf_op jit(solution)/shard_map/ppermute | solution.py:124
  41.9 22.6 %copy-start.3 = (s32[48,64,128]{2,1,0:T(8,128)S(1)}, s32[48,64,128]{2,1,0:T(8,128)}, u32[]{:S(2)}) copy-start(s32[48,64,128]{2,1,0:T(8,128)} %param.8) | copy-start | bytes 4718596
  41.9 22.6 %copy-start.4 = (f32[48,64,128]{2,1,0:T(8,128)S(1)}, f32[48,64,128]{2,1,0:T(8,128)}, u32[]{:S(2)}) copy-start(f32[48,64,128]{2,1,0:T(8,128)} %param.7) | copy-start | bytes 4718596
  42.2 22.3 %collective-permute-start.3 = (bf16[48,64,128]{2,1,0:T(8,128)(2,1)S(1)}, bf16[48,64,128]{2,1,0:T(8,128)(2,1)S(1)}, u32[]{:S(2)}, u32[]{:S(2)}) collective-permute-start(bf16[48,64,128]{2,1,0:T(8,128)(2,1)S(1)} %fusion.7), channel_id=1, source_target_pairs={{2,0},{3,1},{4,2},{5,3},{6,4},{7,5},{8,6},{9,7},{10,8},{11,9},{12,... | collective-permute-start | bytes 2359304 | tf_op jit(solution)/shard_map/ppermute | solution.py:119
  65.5 20.8 %collective-permute-start.4 = (bf16[48,64,128]{2,1,0:T(8,128)(2,1)S(1)}, bf16[48,64,128]{2,1,0:T(8,128)(2,1)S(1)}, u32[]{:S(2)}, u32[]{:S(2)}) collective-permute-start(bf16[48,64,128]{2,1,0:T(8,128)(2,1)S(1)} %get-tuple-element.29.own_in), channel_id=1, source_target_pairs={{0,2},{1,3},{2,4},{3,5},{4,6},{5,7},{6,8},{7,9},{8,10},{9,11},{10,... | collective-permute-start | bytes 2359304 | tf_op jit(solution)/shard_map/ppermute | solution.py:119
  86.4 2.4 %collective-permute-start.5 = (bf16[48,64,128]{2,1,0:T(8,128)(2,1)S(1)}, bf16[48,64,128]{2,1,0:T(8,128)(2,1)S(1)}, u32[]{:S(2)}, u32[]{:S(2)}) collective-permute-start(bf16[48,64,128]{2,1,0:T(8,128)(2,1)S(1)} %broadcast_select_fusion.1), channel_id=1, source_target_pairs={{0,1},{1,0},{2,3},{3,2},{4,5},{5,4},{6,7},{7,6},{8,9},{9,8},{10,11... | collective-permute-start | bytes 2359304 | tf_op jit(solution)/shard_map/ppermute | solution.py:124
  99.4 2.4 %collective-permute-start.6 = (bf16[48,64,128]{2,1,0:T(8,128)(2,1)S(1)}, bf16[48,64,128]{2,1,0:T(8,128)(2,1)S(1)}, u32[]{:S(2)}, u32[]{:S(2)}) collective-permute-start(bf16[48,64,128]{2,1,0:T(8,128)(2,1)S(1)} %get-tuple-element.18), channel_id=1, source_target_pairs={{0,1},{1,0},{2,3},{3,2},{4,5},{5,4},{6,7},{7,6},{8,9},{9,8},{10,11... | collective-permute-start | bytes 2359304 | tf_op jit(solution)/shard_map/ppermute | solution.py:124
  102.0 22.2 %collective-permute-start.7 = (bf16[48,64,128]{2,1,0:T(8,128)(2,1)S(1)}, bf16[48,64,128]{2,1,0:T(8,128)(2,1)S(1)}, u32[]{:S(2)}, u32[]{:S(2)}) collective-permute-start(bf16[48,64,128]{2,1,0:T(8,128)(2,1)S(1)} %fusion.15), channel_id=1, source_target_pairs={{2,0},{3,1},{4,2},{5,3},{6,4},{7,5},{8,6},{9,7},{10,8},{11,9},{12,... | collective-permute-start | bytes 2359304 | tf_op jit(solution)/shard_map/ppermute | solution.py:119
  125.2 58.1 %copy-start.2 = (f32[48,64,128]{2,1,0:T(8,128)}, f32[48,64,128]{2,1,0:T(8,128)S(1)}, u32[]{:S(2)}) copy-start(f32[48,64,128]{2,1,0:T(8,128)S(1)} %get-tuple-element.28.field) | copy-start | bytes 4718596
  125.2 20.8 %collective-permute-start.8 = (bf16[48,64,128]{2,1,0:T(8,128)(2,1)S(1)}, bf16[48,64,128]{2,1,0:T(8,128)(2,1)S(1)}, u32[]{:S(2)}, u32[]{:S(2)}) collective-permute-start(bf16[48,64,128]{2,1,0:T(8,128)(2,1)S(1)} %get-tuple-element.27.own_in), channel_id=1, source_target_pairs={{0,2},{1,3},{2,4},{3,5},{4,6},{5,7},{6,8},{7,9},{8,10},{9,11},{10,... | collective-permute-start | bytes 2359304 | tf_op jit(solution)/shard_map/ppermute | solution.py:119
  146.1 2.4 %collective-permute-start.9 = (bf16[48,64,128]{2,1,0:T(8,128)(2,1)S(1)}, bf16[48,64,128]{2,1,0:T(8,128)(2,1)S(1)}, u32[]{:S(2)}, u32[]{:S(2)}) collective-permute-start(bf16[48,64,128]{2,1,0:T(8,128)(2,1)S(1)} %broadcast_select_fusion), channel_id=1, source_target_pairs={{0,1},{1,0},{2,3},{3,2},{4,5},{5,4},{6,7},{7,6},{8,9},{9,8},{10,11... | collective-permute-start | bytes 2359304 | tf_op jit(solution)/shard_map/ppermute | solution.py:124
  158.5 2.4 %collective-permute-start.10 = (bf16[48,64,128]{2,1,0:T(8,128)(2,1)S(1)}, bf16[48,64,128]{2,1,0:T(8,128)(2,1)S(1)}, u32[]{:S(2)}, u32[]{:S(2)}) collective-permute-start(bf16[48,64,128]{2,1,0:T(8,128)(2,1)S(1)} %get-tuple-element.21), channel_id=1, source_target_pairs={{0,1},{1,0},{2,3},{3,2},{4,5},{5,4},{6,7},{7,6},{8,9},{9,8},{10,11... | collective-permute-start | bytes 2359304 | tf_op jit(solution)/shard_map/ppermute | solution.py:124
  161.1 22.2 %collective-permute-start.11 = (bf16[48,64,128]{2,1,0:T(8,128)(2,1)S(1)}, bf16[48,64,128]{2,1,0:T(8,128)(2,1)S(1)}, u32[]{:S(2)}, u32[]{:S(2)}) collective-permute-start(bf16[48,64,128]{2,1,0:T(8,128)(2,1)S(1)} %fusion.23), channel_id=1, source_target_pairs={{2,0},{3,1},{4,2},{5,3},{6,4},{7,5},{8,6},{9,7},{10,8},{11,9},{12,... | collective-permute-start | bytes 2359304 | tf_op jit(solution)/shard_map/ppermute | solution.py:119

commit v2 on v1

--- a/solution.py
+++ b/solution.py
@@ -9,6 +9,7 @@
 
 leap_size = 0.3
 GROUP = 8
+PARTS = 6
 
 
 def nt(a, b):
@@ -113,56 +114,291 @@
     )(slots, far, near, own, field, cond, whiten)
 
 
-def shifted(value, steps):
+def exchange_kernel(count, parts, back, forward, coefs, *refs):
+    refs = list(refs)
+    take = lambda n: [refs.pop(0) for _ in range(n)]
+    if back:
+        far_hbm, near_hbm, own_hbm, field_hbm, moment_hbm, weight_hbm = take(6)
+        field_hbm_out, moment_hbm_out = take(2)
+    else:
+        (field_hbm,) = take(1)
+    if forward:
+        far_in, near_in, rounded = take(3)
+    if back:
+        far, own, field, moment, weight, other, sent, landed = take(8)
+        load_sem, store_sem = take(2)
+        swap_sem, back_sem = take(2)
+    else:
+        (field,) = take(1)
+        (load_sem,) = take(1)
+    if forward:
+        pass_sem, pair_sem = take(2)
+
+    me = lax.axis_index("blk")
+    odd = lax.rem(me, 2) == 1
+    pair = me + 1 - 2 * lax.rem(me, 2)
+    has_next = me < count - 2
+    has_prev = me >= 2
+    blocks = field.shape[0]
+    size = blocks // parts
+    cut = [pl.ds(c * size, size) for c in range(parts)]
+
+    def load(at, c):
+        source, target = loads[at]
+        return pltpu.make_async_copy(source.at[cut[c]], target.at[cut[c]], load_sem.at[at, c])
+
+    if back:
+        loads = [(far_hbm, far), (own_hbm, own), (field_hbm, field), (moment_hbm, moment), (weight_hbm, weight)]
+    else:
+        loads = [(field_hbm, field)]
+    for at in range(len(loads)):
+        for c in range(parts):
+            load(at, c).start()
+
+    barrier = pltpu.get_barrier_semaphore()
+    pl.semaphore_signal(barrier, inc=1, device_id={"blk": pair}, device_id_type=pl.DeviceIdType.MESH)
+
+    @pl.when(has_next)
+    def _():
+        pl.semaphore_signal(
+            barrier, inc=1, device_id={"blk": me + 2}, device_id_type=pl.DeviceIdType.MESH
+        )
+
+    @pl.when(has_prev)
+    def _():
+        pl.semaphore_signal(
+            barrier, inc=1, device_id={"blk": me - 2}, device_id_type=pl.DeviceIdType.MESH
+        )
+
+    pl.semaphore_wait(barrier, 1 + has_next.astype(jnp.int32) + has_prev.astype(jnp.int32))
+
+    def remote(source, target, sems, c, device):
+        return pltpu.make_async_remote_copy(
+            src_ref=source.at[cut[c]], dst_ref=target.at[cut[c]],
+            send_sem=sems.at[0, c], recv_sem=sems.at[1, c],
+            device_id={"blk": device}, device_id_type=pl.DeviceIdType.MESH,
+        )
+
+    swap = lambda c: remote(near_hbm, other, swap_sem, c, pair)
+    giving = lambda c: remote(sent, landed, back_sem, c, me - 2)
+    passing = lambda c: remote(rounded, far_in, pass_sem, c, me + 2)
+    own_to_pair = lambda c: remote(rounded, near_in, pair_sem, c, pair)
+    far_to_pair = lambda c: remote(far_in, near_in, pair_sem, c, pair)
+
+    def zero(ref):
+        @pl.loop(0, blocks)
+        def _(n):
+            ref[n] = jnp.zeros(ref.shape[1:], ref.dtype)
+
+    if forward:
+        @pl.when(jnp.logical_not(has_prev))
+        def _():
+            zero(far_in)
+
+    if back:
+        for c in range(parts):
+            swap(c).start()
+
+        @pl.when(jnp.logical_not(has_next))
+        def _():
+            zero(landed)
+
+        odd_part = odd.astype(jnp.float32)
+        for c in range(parts):
+            load(0, c).wait()
+            swap(c).wait_recv()
+
+            @pl.loop(c * size, (c + 1) * size)
+            def _(n):
+                sent[n] = (far[n] + odd_part * other[n].astype(jnp.float32)).astype(sent.dtype)
+
+            @pl.when(has_prev)
+            def _():
+                giving(c).start()
+
+    for c in range(parts):
+        for at in range(1 if back else 0, len(loads)):
+            load(at, c).wait()
+        if back:
+            @pl.when(has_next)
+            def _():
+                giving(c).wait_recv()
+
+        @pl.loop(c * size, (c + 1) * size)
+        def _(n):
+            x = field[n]
+            if back:
+                total = own[n] + (1.0 - odd_part) * other[n].astype(jnp.float32)
+                total = total + landed[n].astype(jnp.float32)
+                grad = total + jnp.exp(x) - weight[n].astype(jnp.float32)
+                m = moment[n] - coefs[0] * grad
+                x = x + coefs[1] * m if coefs[1] else x
+                moment[n] = m
+                if coefs[1]:
+                    field[n] = x
+            if forward:
+                rounded[n] = x.astype(rounded.dtype)
+
+        if forward:
+            @pl.when(has_next)
+            def _():
+                passing(c).start()
+
+            @pl.when(jnp.logical_not(odd))
+            def _():
+                own_to_pair(c).start()
+        if back:
+            pltpu.make_async_copy(moment.at[cut[c]], moment_hbm_out.at[cut[c]], store_sem.at[0, c]).start()
+            pltpu.make_async_copy(field.at[cut[c]], field_hbm_out.at[cut[c]], store_sem.at[1, c]).start()
+
+    if forward:
+        for c in range(parts):
+            @pl.when(has_prev)
+            def _():
+                passing(c).wait_recv()
+
+            @pl.when(odd)
+            def _():
+                far_to_pair(c).start()
+
+        for c in range(parts):
+            own_to_pair(c).wait_recv()
+            own_to_pair(c).wait_send()
+
+            @pl.when(has_next)
+            def _():
+                passing(c).wait_send()
+
+    if back:
+        for c in range(parts):
+            swap(c).wait_send()
+
+            @pl.when(has_prev)
+            def _():
+                giving(c).wait_send()
+
+            pltpu.make_async_copy(moment.at[cut[c]], moment_hbm_out.at[cut[c]], store_sem.at[0, c]).wait()
+            pltpu.make_async_copy(field.at[cut[c]], field_hbm_out.at[cut[c]], store_sem.at[1, c]).wait()
+
+
+def exchange(operands, back, forward, coefs, collective_id):
     count = lax.axis_size("blk")
-    leading, last = (max(0, -steps), min(count, count - steps))
-    return lax.ppermute(value, "blk", [(source, source + steps) for source in range(leading, last)])
-
-
-def swapped(value):
+    shape = operands[-1].shape
+    blocks = shape[0]
+    parts = PARTS if blocks % PARTS == 0 else 1
+    hbm = pl.BlockSpec(memory_space=pl.ANY)
+    vmem = pl.BlockSpec(memory_space=pltpu.VMEM)
+    full, half = jnp.float32, jnp.bfloat16
+    out_shape, out_specs, scratch = [], [], []
+    if back:
+        out_shape += [jax.ShapeDtypeStruct(shape, full)] * 2
+        out_specs += [hbm] * 2
+    if forward:
+        out_shape += [jax.ShapeDtypeStruct(shape, half)] * 3
+        out_specs += [vmem] * 3
+    sems = lambda n: pltpu.SemaphoreType.DMA((n, parts))
+    if back:
+        scratch += [pltpu.VMEM(shape, full)] * 4 + [pltpu.VMEM(shape, jnp.int32)]
+        scratch += [pltpu.VMEM(shape, half)] * 3
+        scratch += [sems(5), sems(2), sems(2), sems(2)]
+    else:
+        scratch += [pltpu.VMEM(shape, full), sems(1)]
+    if forward:
+        scratch += [sems(2), sems(2)]
+    return pl.pallas_call(
+        functools.partial(exchange_kernel, count, parts, back, forward, coefs),
+        in_specs=[hbm] * len(operands),
+        out_specs=out_specs,
+        out_shape=out_shape,
+        scratch_shapes=scratch,
+        compiler_params=pltpu.CompilerParams(
+            vmem_limit_bytes=40 * 2**20, collective_id=collective_id, has_side_effects=True
+        ),
+        name="exchange",
+    )(*operands)
+
+
+def sum_kernel(count, value, total, slots, send_sem, recv_sem):
+    me = lax.axis_index("blk")
+    barrier = pltpu.get_barrier_semaphore()
+
+    @pl.loop(1, count)
+    def _(d):
+        pl.semaphore_signal(
+            barrier, inc=1, device_id={"blk": lax.rem(me + d, count)},
+            device_id_type=pl.DeviceIdType.MESH,
+        )
+
+    pl.semaphore_wait(barrier, count - 1)
+
+    def copy(d):
+        return pltpu.make_async_remote_copy(
+            src_ref=value, dst_ref=slots.at[d], send_sem=send_sem.at[d], recv_sem=recv_sem.at[d],
+            device_id={"blk": lax.rem(me + d, count)}, device_id_type=pl.DeviceIdType.MESH,
+        )
+
+    @pl.loop(1, count)
+    def _(d):
+        copy(d).start()
+
+    total[...] = value[...]
+
+    @pl.loop(1, count)
+    def _(d):
+        copy(d).wait()
+        total[...] += slots[d]
+
+
+def summed(value, collective_id):
     count = lax.axis_size("blk")
-    return lax.ppermute(value, "blk", [(source, source ^ 1) for source in range(count)])
+    tile = jnp.zeros((8, 128), jnp.float32).at[0, : value.shape[0]].set(value)
+    total = pl.pallas_call(
+        functools.partial(sum_kernel, count),
+        in_specs=[pl.BlockSpec(memory_space=pltpu.VMEM)],
+        out_specs=pl.BlockSpec(memory_space=pltpu.VMEM),
+        out_shape=jax.ShapeDtypeStruct(tile.shape, jnp.float32),
+        scratch_shapes=[
+            pltpu.VMEM((count, 8, 128), jnp.float32),
+            pltpu.SemaphoreType.DMA((count,)),
+            pltpu.SemaphoreType.DMA((count,)),
+        ],
+        compiler_params=pltpu.CompilerParams(collective_id=collective_id, has_side_effects=True),
+        name="summed",
+    )(tile)
+    return total[0, : value.shape[0]]
 
 
 def per_device(position, momentum, counts, neighbours, cond_factor, whiten):
     blocks = position.shape[0]
-    me = lax.axis_index("blk")
-    odd = lax.rem(me, 2) == 1
-    first_block = (me - 2) * blocks
+    first_block = (lax.axis_index("blk") - 2) * blocks
     slots = jnp.where(
         neighbours >= 0, jnp.clip(neighbours - first_block, 0, 3 * blocks - 1), 3 * blocks
     ).reshape(-1)
     weight = counts.astype(jnp.float32)
-
-    def gradient(field):
-        rounded = field.astype(jnp.bfloat16)
-        farther = shifted(rounded, 2)
-        earlier = swapped(jnp.where(odd, farther, rounded))
-        far, near, own, square = terms(
-            slots, farther, earlier, rounded, field, cond_factor, whiten
-        )
-        other = swapped(near).astype(jnp.float32)
-        back = (far + jnp.where(odd, other, 0.0)).astype(jnp.bfloat16)
-        own = own + jnp.where(odd, 0.0, other)
-        grad = own + shifted(back, -2).astype(jnp.float32) + jnp.exp(field) - weight
-        return grad, square
+    h = leap_size
+
+    def pieces(near_by, field):
+        return terms(slots, *near_by, field, cond_factor, whiten)
 
     def local_cell(field):
         return jnp.exp(field) - weight * field
 
-    grad, square_start = gradient(position)
-    moment = momentum - 0.5 * leap_size * grad
-    field = position + leap_size * moment
-    grad, _ = gradient(field)
-    moment = moment - leap_size * grad
-    field = field + leap_size * moment
-    grad, square_end = gradient(field)
-    moment = moment - 0.5 * leap_size * grad
+    near_by = exchange((position,), False, True, None, 1)
+    far, near, own, square_start = pieces(near_by, position)
+    field, moment, *near_by = exchange(
+        (far, near, own, position, momentum, counts), True, True, (0.5 * h, h), 2
+    )
+    far, near, own, _ = pieces(near_by, field)
+    field, moment, *near_by = exchange(
+        (far, near, own, field, moment, counts), True, True, (h, h), 3
+    )
+    far, near, own, square_end = pieces(near_by, field)
+    _, moment = exchange((far, near, own, field, moment, counts), True, False, (0.5 * h, 0.0), 4)
     change = (
         local_cell(field) + 0.5 * moment * moment - local_cell(position) - 0.5 * momentum * momentum
     )
     change = jnp.sum(change, axis=0) + 0.5 * (square_end - square_start)
-    total = lax.psum(jnp.sum(change, axis=1), "blk")
+    total = summed(jnp.sum(change, axis=1), 5)
     return (field, moment, total)
 
 

time: 220 us -> 183 us (0.83)
  Pallas kernels: 31.4 us -> 174 us
  waiting for transfers between devices: 125 us -> 0 us
  blocking collectives: 32.6 us -> 0 us
  starting transfers between devices: 19.6 us -> 0 us
  other arithmetic: 9.65 us -> 1.78 us
  local copies, waits for them, and re-layouts: 0.22 us -> 5.71 us
    pallas_call x0 -> x5, Pallas kernels: none -> 143 us  [the longest x4 133 us: exchange(): pl.pallas_call(functools.partial(exchange_kernel, count, parts, back, for...]
    ppermute x12 -> x0, waiting for transfers between devices: 125 us -> none  [the longest x6 111 us: shifted(): lax.ppermute(value, 'blk', [(source, source + steps) for source in range(...]
    psum x1 -> x0, blocking collectives: 32.6 us -> none  [per_device(): total = lax.psum(jnp.sum(change, axis=1), 'blk')]
    ppermute x12 -> x0, starting transfers between devices: 19.6 us -> none  [the longest x6 19 us: shifted(): lax.ppermute(value, 'blk', [(source, source + steps) for source in range(...]
    convert_element_type x6 -> x0, other arithmetic: 5.37 us -> none  [the longest x3 4.59 us: gradient(): rounded = field.astype(jnp.bfloat16)]
    unnamed x12, local copies, waits for them, and re-layouts: 0.03 us -> 3.71 us
  transfers between devices with their start and end apart: 12 -> 0, of which waited for: 12 -> 0; matrix products, arithmetic and copies ran while one was open for 0% -> 0% of each run, Pallas kernels for 0% -> 0%
where the time goes in v2:
time: 183 us; the launch traced here: 182 us
  Pallas kernels  174 us (95%)
  local copies, waits for them, and re-layouts  5.71 us (3%)
    pallas_call x4, Pallas kernels, exchange(): pl.pallas_call(functools.partial(exchange_kernel, count, parts, back, for...  133 us
    pallas_call x3, Pallas kernels, terms(): pl.pallas_call(functools.partial(terms_kernel, group), grid_spec=pltpu.Pr...  31 us
    pallas_call x1, Pallas kernels, summed(): pl.pallas_call(functools.partial(sum_kernel, count), in_specs=[pl.BlockSp...  10.4 us
    unnamed x12, local copies, waits for them, and re-layouts  3.71 us

profile of v2, /device:TPU:0, one launch (start us, length us, event | category | flops | bytes accessed | tf_op | source)
XLA Modules:
  0.0 182.3 jit_solution(8829898684429655998)
XLA Ops:
  0.6 0.7 clamp_select_fusion
  1.3 0.1 copy.9
  1.4 0.1 reshape.39.slots
  1.5 0.0 copy-start
  1.5 1.4 copy-done
  2.9 20.5 %exchange.4 = (bf16[48,64,128]{2,1,0:T(8,128)(2,1)S(1)}, bf16[48,64,128]{2,1,0:T(8,128)(2,1)S(1)}, bf16[48,64,128]{2,1,0:T(8,128)(2,1)S(1)}) custom-call(f32[48,64,128]{2,1,0:T(8,128)S(1)} %copy-done), custom_call_target="tpu_custom_call" | custom-call | tf_op jit(solution)/shard_map/exchange/pallas_call | solution.py:308
  23.4 0.0 copy-done.3
  23.4 0.0 copy-start.2
  23.4 0.0 copy-start.4
  23.4 10.3 %terms.3 = (f32[48,64,128]{2,1,0:T(8,128)S(1)}, bf16[48,64,128]{2,1,0:T(8,128)(2,1)S(1)}, f32[48,64,128]{2,1,0:T(8,128)S(1)}, f32[64,128]{1,0:T(8,128)S(1)}) custom-call(s32[192]{0:T(256)S(1)} %reshape.39.slots, bf16[48,64,128]{2,1,0:T(8,128)(2,1)S(1)} %get-tuple-element.40.far_in, bf16[48,64,128]{2,1,0:T(8,128)(2,1)S(1)} %get-tuple-element.41.near_in, ...), custom_call_target="tpu_custom_call" | custom-call | flops 1006632960 | bytes 20971520 | tf_op jit(solution)/shard_map/terms/pallas_call | solution.py:85
  33.8 0.0 copy-done.2
  33.8 40.2 %exchange.5 = (f32[48,64,128]{2,1,0:T(8,128)S(1)}, f32[48,64,128]{2,1,0:T(8,128)S(1)}, bf16[48,64,128]{2,1,0:T(8,128)(2,1)S(1)}, bf16[48,64,128]{2,1,0:T(8,128)(2,1)S(1)}, bf16[48,64,128]{2,1,0:T(8,128)(2,1)S(1)}) custom-call(f32[48,64,128]{2,1,0:T(8,128)S(1)} %get-tuple-element.43.refs_0_, bf16[48,64,128]{2,1,0:T(8,128)(2,1)S(1)} %get-tuple-element.44.refs_1_, ...), custom_call_target="tpu_custom_call" | custom-call | tf_op jit(solution)/shard_map/exchange/pallas_call | solution.py:308
  74.0 10.6 %terms.4 = (f32[48,64,128]{2,1,0:T(8,128)S(1)}, bf16[48,64,128]{2,1,0:T(8,128)(2,1)S(1)}, f32[48,64,128]{2,1,0:T(8,128)S(1)}, f32[64,128]{1,0:T(8,128)}) custom-call(s32[192]{0:T(256)S(1)} %reshape.39.slots, bf16[48,64,128]{2,1,0:T(8,128)(2,1)S(1)} %get-tuple-element.46.far_in, bf16[48,64,128]{2,1,0:T(8,128)(2,1)S(1)} %get-tuple-element.47.near_in, ...), custom_call_target="tpu_custom_call" | custom-call | flops 1006632960 | bytes 20971520 | tf_op jit(solution)/shard_map/terms/pallas_call | solution.py:85
  84.7 46.3 %exchange.6 = (f32[48,64,128]{2,1,0:T(8,128)S(1)}, f32[48,64,128]{2,1,0:T(8,128)S(1)}, bf16[48,64,128]{2,1,0:T(8,128)(2,1)S(1)}, bf16[48,64,128]{2,1,0:T(8,128)(2,1)S(1)}, bf16[48,64,128]{2,1,0:T(8,128)(2,1)S(1)}) custom-call(f32[48,64,128]{2,1,0:T(8,128)S(1)} %get-tuple-element.50.refs_0_, bf16[48,64,128]{2,1,0:T(8,128)(2,1)S(1)} %get-tuple-element.51.refs_1_, ...), custom_call_target="tpu_custom_call" | custom-call | tf_op jit(solution)/shard_map/exchange/pallas_call | solution.py:308
  131.0 10.0 %terms.5 = (f32[48,64,128]{2,1,0:T(8,128)S(1)}, bf16[48,64,128]{2,1,0:T(8,128)(2,1)S(1)}, f32[48,64,128]{2,1,0:T(8,128)S(1)}, f32[64,128]{1,0:T(8,128)S(1)}) custom-call(s32[192]{0:T(256)S(1)} %reshape.39.slots, bf16[48,64,128]{2,1,0:T(8,128)(2,1)S(1)} %get-tuple-element.55.far_in, bf16[48,64,128]{2,1,0:T(8,128)(2,1)S(1)} %get-tuple-element.56.near_in, ...), custom_call_target="tpu_custom_call" | custom-call | flops 1006632960 | bytes 20971520 | tf_op jit(solution)/shard_map/terms/pallas_call | solution.py:85
  141.1 0.0 copy-start.1
  141.1 25.6 %exchange.7 = (f32[48,64,128]{2,1,0:T(8,128)}, f32[48,64,128]{2,1,0:T(8,128)S(1)}) custom-call(f32[48,64,128]{2,1,0:T(8,128)S(1)} %get-tuple-element.58.refs_0_, bf16[48,64,128]{2,1,0:T(8,128)(2,1)S(1)} %get-tuple-element.59.refs_1_, f32[48,64,128]{2,1,0:T(8,128)S(1)} %get-tuple-element.60.refs_2_, f32[48,64,128]{2,1,0:T(8,128)S(1)} %get-tuple-element.68.field.refs_3_, ...), custom_call_target="tpu_custom_call" | custom-call | tf_op jit(solution)/shard_map/exchange/pallas_call | solution.py:308
  166.7 1.0 fusion.3
  167.7 0.1 add_reduce_fusion
  167.8 0.6 scatter.4.value
  168.4 10.4 %summed.1 = f32[8,128]{1,0:T(8,128)} custom-call(f32[8,128]{1,0:T(8,128)} %scatter.4.value), custom_call_target="tpu_custom_call" | custom-call | tf_op jit(solution)/shard_map/summed/pallas_call | solution.py:355
  178.8 1.2 slice_bitcast_fusion
  180.0 1.1 copy.12
  181.1 1.1 copy.13
  (3 shorter events, 0.0 us)
Async XLA Ops:
  1.5 1.4 copy-start
  2.9 20.5 %copy-start.3 = (bf16[48,128,128]{2,1,0:T(8,128)(2,1)S(1)}, bf16[48,128,128]{2,1,0:T(8,128)(2,1)}, u32[]{:S(2)}) copy-start(bf16[48,128,128]{2,1,0:T(8,128)(2,1)} %whiten.5) | copy-start | bytes 4718596
  23.4 10.4 %copy-start.2 = (s32[48,64,128]{2,1,0:T(8,128)S(1)}, s32[48,64,128]{2,1,0:T(8,128)}, u32[]{:S(2)}) copy-start(s32[48,64,128]{2,1,0:T(8,128)} %refs_5_.5) | copy-start | bytes 4718596
  23.4 10.3 %copy-start.4 = (f32[48,64,128]{2,1,0:T(8,128)S(1)}, f32[48,64,128]{2,1,0:T(8,128)}, u32[]{:S(2)}) copy-start(f32[48,64,128]{2,1,0:T(8,128)} %refs_4_.1) | copy-start | bytes 4718596
  141.1 25.7 %copy-start.1 = (f32[48,64,128]{2,1,0:T(8,128)S(1)}, f32[48,64,128]{2,1,0:T(8,128)}, u32[]{:S(2)}) copy-start(f32[48,64,128]{2,1,0:T(8,128)} %refs_3_.1) | copy-start | bytes 4718596

commit v3 on v2

--- a/solution.py
+++ b/solution.py
@@ -22,9 +22,11 @@
 
 def terms_kernel(
     group, slots, far_in, near_in, own_in, field, cond, whiten,
-    far_out, near_out, own_out, square_out,
-    window, acc, sems,
+    far_out, near_out, own_out, square_out, *rest,
 ):
+    window, acc, sems = rest[-3:]
+    if len(rest) == 4:
+        rest[0][...] = field[...]
     blocks = far_in.shape[0]
     step = pl.program_id(0)
     steps = pl.num_programs(0)
@@ -70,14 +72,22 @@
 
     @pl.when(step == steps - 1)
     def _():
+        copies = [
+            pltpu.make_async_copy(acc.at[pl.ds(0, blocks)], far_out, sems.at[0]),
+            pltpu.make_async_copy(acc.at[pl.ds(2 * blocks, blocks)], own_out, sems.at[1]),
+        ]
+        for copy in copies:
+            copy.start()
+
         @pl.loop(0, blocks)
         def _(at):
-            far_out[at] = acc[at]
             near_out[at] = acc[blocks + at].astype(near_out.dtype)
-            own_out[at] = acc[2 * blocks + at]
-
-
-def terms(slots, far, near, own, field, cond, whiten):
+
+        for copy in copies:
+            copy.wait()
+
+
+def terms(slots, far, near, own, field, cond, whiten, keep=False):
     blocks, chains, points = field.shape
     group = GROUP if blocks % GROUP == 0 else 1
     whole = pl.BlockSpec((blocks, chains, points), lambda s, i: (0, 0, 0))
@@ -93,7 +103,10 @@
                 pl.BlockSpec((group, 4, points, points), lambda s, i: (s, 0, 0, 0)),
                 pl.BlockSpec((group, points, points), lambda s, i: (s, 0, 0)),
             ],
-            out_specs=[whole, whole, whole, pl.BlockSpec((chains, points), lambda s, i: (0, 0))],
+            out_specs=[
+                hbm, whole, hbm, pl.BlockSpec((chains, points), lambda s, i: (0, 0)),
+                pl.BlockSpec((group, chains, points), lambda s, i: (s, 0, 0)),
+            ][: 5 if keep else 4],
             scratch_shapes=[
                 pltpu.VMEM((3 * blocks + 1, chains, points), jnp.bfloat16),
                 pltpu.VMEM((3 * blocks + 1, chains, points), jnp.float32),
@@ -105,7 +118,8 @@
             jax.ShapeDtypeStruct(field.shape, jnp.bfloat16),
             jax.ShapeDtypeStruct(field.shape, jnp.float32),
             jax.ShapeDtypeStruct((chains, points), jnp.float32),
-        ],
+            jax.ShapeDtypeStruct(field.shape, jnp.float32),
+        ][: 5 if keep else 4],
         compiler_params=pltpu.CompilerParams(vmem_limit_bytes=40 * 2**20),
         cost_estimate=pl.CostEstimate(
             flops=20 * blocks * chains * points * points, bytes_accessed=20 * 2**20, transcendentals=0
@@ -114,16 +128,22 @@
     )(slots, far, near, own, field, cond, whiten)
 
 
-def exchange_kernel(count, parts, back, forward, coefs, *refs):
+def exchange_kernel(count, parts, back, forward, energy, coefs, *refs):
     refs = list(refs)
     take = lambda n: [refs.pop(0) for _ in range(n)]
     if back:
         far_hbm, near_hbm, own_hbm, field_hbm, moment_hbm, weight_hbm = take(6)
-        field_hbm_out, moment_hbm_out = take(2)
+        if energy:
+            start_hbm, push_hbm, square = take(3)
+        moment_hbm_out = take(1)[0]
+        if forward:
+            field_hbm_out = take(1)[0]
     else:
         (field_hbm,) = take(1)
     if forward:
-        far_in, near_in, rounded = take(3)
+        forward_out = take(3)
+    if energy:
+        (total_out,) = take(1)
     if back:
         far, own, field, moment, weight, other, sent, landed = take(8)
         load_sem, store_sem = take(2)
@@ -132,7 +152,10 @@
         (field,) = take(1)
         (load_sem,) = take(1)
     if forward:
-        pass_sem, pair_sem = take(2)
+        far_in, near_in, rounded = take(3)
+        pass_sem, pair_sem, out_sem = take(3)
+    if energy:
+        start, push, gain, slots, sum_send, sum_recv = take(6)
 
     me = lax.axis_index("blk")
     odd = lax.rem(me, 2) == 1
@@ -149,6 +172,8 @@
 
     if back:
         loads = [(far_hbm, far), (own_hbm, own), (field_hbm, field), (moment_hbm, moment), (weight_hbm, weight)]
+        if energy:
+            loads += [(start_hbm, start), (push_hbm, push)]
     else:
         loads = [(field_hbm, field)]
     for at in range(len(loads)):
@@ -170,7 +195,15 @@
             barrier, inc=1, device_id={"blk": me - 2}, device_id_type=pl.DeviceIdType.MESH
         )
 
-    pl.semaphore_wait(barrier, 1 + has_next.astype(jnp.int32) + has_prev.astype(jnp.int32))
+    if energy:
+        @pl.loop(1, count)
+        def _(d):
+            pl.semaphore_signal(
+                barrier, inc=1, device_id={"blk": lax.rem(me + d, count)},
+                device_id_type=pl.DeviceIdType.MESH,
+            )
+
+    pl.semaphore_wait(barrier, (count if energy else 1) + has_next.astype(jnp.int32) + has_prev.astype(jnp.int32))
 
     def remote(source, target, sems, c, device):
         return pltpu.make_async_remote_copy(
@@ -185,6 +218,11 @@
     own_to_pair = lambda c: remote(rounded, near_in, pair_sem, c, pair)
     far_to_pair = lambda c: remote(far_in, near_in, pair_sem, c, pair)
 
+    def keep(at, c):
+        return pltpu.make_async_copy(
+            (far_in, near_in, rounded)[at].at[cut[c]], forward_out[at].at[cut[c]], out_sem.at[at, c]
+        )
+
     def zero(ref):
         @pl.loop(0, blocks)
         def _(n):
@@ -216,6 +254,8 @@
             def _():
                 giving(c).start()
 
+    if energy:
+        gain[...] = 0.5 * square[...]
     for c in range(parts):
         for at in range(1 if back else 0, len(loads)):
             load(at, c).wait()
@@ -234,12 +274,20 @@
                 m = moment[n] - coefs[0] * grad
                 x = x + coefs[1] * m if coefs[1] else x
                 moment[n] = m
+                if energy:
+                    w, x0, m0 = weight[n].astype(jnp.float32), start[n], push[n]
+                    gain[...] += (
+                        jnp.exp(x) - w * x + 0.5 * m * m
+                        - (jnp.exp(x0) - w * x0 + 0.5 * m0 * m0)
+                    )
                 if coefs[1]:
                     field[n] = x
             if forward:
                 rounded[n] = x.astype(rounded.dtype)
 
         if forward:
+            keep(2, c).start()
+
             @pl.when(has_next)
             def _():
                 passing(c).start()
@@ -249,7 +297,8 @@
                 own_to_pair(c).start()
         if back:
             pltpu.make_async_copy(moment.at[cut[c]], moment_hbm_out.at[cut[c]], store_sem.at[0, c]).start()
-            pltpu.make_async_copy(field.at[cut[c]], field_hbm_out.at[cut[c]], store_sem.at[1, c]).start()
+            if forward:
+                pltpu.make_async_copy(field.at[cut[c]], field_hbm_out.at[cut[c]], store_sem.at[1, c]).start()
 
     if forward:
         for c in range(parts):
@@ -261,14 +310,48 @@
             def _():
                 far_to_pair(c).start()
 
+            keep(0, c).start()
+
         for c in range(parts):
             own_to_pair(c).wait_recv()
+            keep(1, c).start()
+
+        for c in range(parts):
+            for at in range(3):
+                keep(at, c).wait()
             own_to_pair(c).wait_send()
 
             @pl.when(has_next)
             def _():
                 passing(c).wait_send()
 
+    if energy:
+        def spread(d):
+            return pltpu.make_async_remote_copy(
+                src_ref=slots.at[0], dst_ref=slots.at[d],
+                send_sem=sum_send.at[d], recv_sem=sum_recv.at[d],
+                device_id={"blk": lax.rem(me + d, count)}, device_id_type=pl.DeviceIdType.MESH,
+            )
+
+        chains, points = gain.shape
+        lanes = slots.shape[2]
+        column = jnp.broadcast_to(jnp.sum(gain[...], axis=1, keepdims=True), (chains, lanes))
+        row = lax.broadcasted_iota(jnp.int32, (chains, lanes), 0)
+        lane = lax.broadcasted_iota(jnp.int32, (chains, lanes), 1)
+        line = jnp.sum(jnp.where(row == lane, column, 0.0), axis=0, keepdims=True)
+        slots[0] = jnp.broadcast_to(line, slots.shape[1:])
+
+        @pl.loop(1, count)
+        def _(d):
+            spread(d).start()
+
+        total_out[...] = slots[0]
+
+        @pl.loop(1, count)
+        def _(d):
+            spread(d).wait()
+            total_out[...] += slots[d]
+
     if back:
         for c in range(parts):
             swap(c).wait_send()
@@ -278,12 +361,14 @@
                 giving(c).wait_send()
 
             pltpu.make_async_copy(moment.at[cut[c]], moment_hbm_out.at[cut[c]], store_sem.at[0, c]).wait()
-            pltpu.make_async_copy(field.at[cut[c]], field_hbm_out.at[cut[c]], store_sem.at[1, c]).wait()
-
-
-def exchange(operands, back, forward, coefs, collective_id):
+            if forward:
+                pltpu.make_async_copy(field.at[cut[c]], field_hbm_out.at[cut[c]], store_sem.at[1, c]).wait()
+
+
+def exchange(operands, back, forward, coefs, collective_id, energy=False):
     count = lax.axis_size("blk")
-    shape = operands[-1].shape
+    shape = operands[5 if back else 0].shape
+    lanes = -(-shape[1] // 128) * 128
     blocks = shape[0]
     parts = PARTS if blocks % PARTS == 0 else 1
     hbm = pl.BlockSpec(memory_space=pl.ANY)
@@ -291,23 +376,32 @@
     full, half = jnp.float32, jnp.bfloat16
     out_shape, out_specs, scratch = [], [], []
     if back:
-        out_shape += [jax.ShapeDtypeStruct(shape, full)] * 2
-        out_specs += [hbm] * 2
+        out_shape += [jax.ShapeDtypeStruct(shape, full)] * (2 if forward else 1)
+        out_specs += [hbm] * (2 if forward else 1)
     if forward:
         out_shape += [jax.ShapeDtypeStruct(shape, half)] * 3
-        out_specs += [vmem] * 3
+        out_specs += [hbm] * 3
+    if energy:
+        out_shape += [jax.ShapeDtypeStruct((8, lanes), full)]
+        out_specs += [vmem]
     sems = lambda n: pltpu.SemaphoreType.DMA((n, parts))
     if back:
         scratch += [pltpu.VMEM(shape, full)] * 4 + [pltpu.VMEM(shape, jnp.int32)]
         scratch += [pltpu.VMEM(shape, half)] * 3
-        scratch += [sems(5), sems(2), sems(2), sems(2)]
+        scratch += [sems(7 if energy else 5), sems(2), sems(2), sems(2)]
     else:
         scratch += [pltpu.VMEM(shape, full), sems(1)]
     if forward:
-        scratch += [sems(2), sems(2)]
+        scratch += [pltpu.VMEM(shape, half)] * 3 + [sems(2), sems(2), sems(3)]
+    if energy:
+        scratch += [
+            pltpu.VMEM(shape, full), pltpu.VMEM(shape, full), pltpu.VMEM(shape[1:], full),
+            pltpu.VMEM((count, 8, lanes), full),
+            pltpu.SemaphoreType.DMA((count,)), pltpu.SemaphoreType.DMA((count,)),
+        ]
     return pl.pallas_call(
-        functools.partial(exchange_kernel, count, parts, back, forward, coefs),
-        in_specs=[hbm] * len(operands),
+        functools.partial(exchange_kernel, count, parts, back, forward, energy, coefs),
+        in_specs=[hbm] * 8 + [vmem] if energy else [hbm] * len(operands),
         out_specs=out_specs,
         out_shape=out_shape,
         scratch_shapes=scratch,
@@ -318,88 +412,32 @@
     )(*operands)
 
 
-def sum_kernel(count, value, total, slots, send_sem, recv_sem):
-    me = lax.axis_index("blk")
-    barrier = pltpu.get_barrier_semaphore()
-
-    @pl.loop(1, count)
-    def _(d):
-        pl.semaphore_signal(
-            barrier, inc=1, device_id={"blk": lax.rem(me + d, count)},
-            device_id_type=pl.DeviceIdType.MESH,
-        )
-
-    pl.semaphore_wait(barrier, count - 1)
-
-    def copy(d):
-        return pltpu.make_async_remote_copy(
-            src_ref=value, dst_ref=slots.at[d], send_sem=send_sem.at[d], recv_sem=recv_sem.at[d],
-            device_id={"blk": lax.rem(me + d, count)}, device_id_type=pl.DeviceIdType.MESH,
-        )
-
-    @pl.loop(1, count)
-    def _(d):
-        copy(d).start()
-
-    total[...] = value[...]
-
-    @pl.loop(1, count)
-    def _(d):
-        copy(d).wait()
-        total[...] += slots[d]
-
-
-def summed(value, collective_id):
-    count = lax.axis_size("blk")
-    tile = jnp.zeros((8, 128), jnp.float32).at[0, : value.shape[0]].set(value)
-    total = pl.pallas_call(
-        functools.partial(sum_kernel, count),
-        in_specs=[pl.BlockSpec(memory_space=pltpu.VMEM)],
-        out_specs=pl.BlockSpec(memory_space=pltpu.VMEM),
-        out_shape=jax.ShapeDtypeStruct(tile.shape, jnp.float32),
-        scratch_shapes=[
-            pltpu.VMEM((count, 8, 128), jnp.float32),
-            pltpu.SemaphoreType.DMA((count,)),
-            pltpu.SemaphoreType.DMA((count,)),
-        ],
-        compiler_params=pltpu.CompilerParams(collective_id=collective_id, has_side_effects=True),
-        name="summed",
-    )(tile)
-    return total[0, : value.shape[0]]
-
-
 def per_device(position, momentum, counts, neighbours, cond_factor, whiten):
     blocks = position.shape[0]
     first_block = (lax.axis_index("blk") - 2) * blocks
     slots = jnp.where(
         neighbours >= 0, jnp.clip(neighbours - first_block, 0, 3 * blocks - 1), 3 * blocks
     ).reshape(-1)
-    weight = counts.astype(jnp.float32)
     h = leap_size
 
-    def pieces(near_by, field):
-        return terms(slots, *near_by, field, cond_factor, whiten)
-
-    def local_cell(field):
-        return jnp.exp(field) - weight * field
+    def pieces(near_by, field, keep=False):
+        return terms(slots, *near_by, field, cond_factor, whiten, keep)
 
     near_by = exchange((position,), False, True, None, 1)
     far, near, own, square_start = pieces(near_by, position)
-    field, moment, *near_by = exchange(
+    moment, field, *near_by = exchange(
         (far, near, own, position, momentum, counts), True, True, (0.5 * h, h), 2
     )
     far, near, own, _ = pieces(near_by, field)
-    field, moment, *near_by = exchange(
+    moment, field, *near_by = exchange(
         (far, near, own, field, moment, counts), True, True, (h, h), 3
     )
-    far, near, own, square_end = pieces(near_by, field)
-    _, moment = exchange((far, near, own, field, moment, counts), True, False, (0.5 * h, 0.0), 4)
-    change = (
-        local_cell(field) + 0.5 * moment * moment - local_cell(position) - 0.5 * momentum * momentum
+    far, near, own, square_end, field_end = pieces(near_by, field, True)
+    moment, total = exchange(
+        (far, near, own, field, moment, counts, position, momentum, square_end - square_start),
+        True, False, (0.5 * h, 0.0), 4, True,
     )
-    change = jnp.sum(change, axis=0) + 0.5 * (square_end - square_start)
-    total = summed(jnp.sum(change, axis=1), 5)
-    return (field, moment, total)
+    return (field_end, moment, total[0, : position.shape[1]])
 
 
 def solution(mesh):

time: 183 us -> 181 us (0.989)
  local copies, waits for them, and re-layouts: 5.71 us -> 3.28 us
  Pallas kernels: 174 us -> 176 us
    pallas_call x4, Pallas kernels: 133 us -> 144 us  [exchange(): pl.pallas_call(functools.partial(exchange_kernel, count, parts, back, for...]
    pallas_call x1 -> x0, Pallas kernels: 10.4 us -> none  [summed(): pl.pallas_call(functools.partial(sum_kernel, count), in_specs=[pl.BlockSp...]
    unnamed x12 -> x11, local copies, waits for them, and re-layouts: 3.71 us -> 2.57 us
where the time goes in v3:
time: 181 us
  Pallas kernels  176 us (97%)
  local copies, waits for them, and re-layouts  3.28 us (2%)
    pallas_call x4, Pallas kernels, exchange(): pl.pallas_call(functools.partial(exchange_kernel, count, parts, back, for...  144 us
    pallas_call x3, Pallas kernels, terms(): pl.pallas_call(functools.partial(terms_kernel, group), grid_spec=pltpu.Pr...  32.1 us

profile of v3, /device:TPU:0, one launch (start us, length us, event | category | flops | bytes accessed | tf_op | source)
XLA Modules:
  0.0 180.8 jit_solution(884172395827953545)
XLA Ops:
  0.6 0.7 clamp_select_fusion
  1.3 0.1 copy.9
  1.4 0.1 reshape.9.slots
  1.5 0.0 copy-start
  1.5 1.4 copy-done
  2.9 0.0 copy-start.2
  2.9 20.8 %exchange.4 = (bf16[48,64,128]{2,1,0:T(8,128)(2,1)S(1)}, bf16[48,64,128]{2,1,0:T(8,128)(2,1)S(1)}, bf16[48,64,128]{2,1,0:T(8,128)(2,1)S(1)}) custom-call(f32[48,64,128]{2,1,0:T(8,128)S(1)} %copy-done), custom_call_target="tpu_custom_call" | custom-call | tf_op jit(solution)/shard_map/exchange/pallas_call | solution.py:402
  23.7 0.0 copy-done.2
  23.8 0.0 copy-start.3
  23.8 0.0 copy-start.4
  23.8 10.4 %terms.3 = (f32[48,64,128]{2,1,0:T(8,128)S(1)}, bf16[48,64,128]{2,1,0:T(8,128)(2,1)S(1)}, f32[48,64,128]{2,1,0:T(8,128)S(1)}, f32[64,128]{1,0:T(8,128)S(1)}) custom-call(s32[192]{0:T(256)S(1)} %reshape.9.slots, bf16[48,64,128]{2,1,0:T(8,128)(2,1)S(1)} %get-tuple-element.30.far_in, bf16[48,64,128]{2,1,0:T(8,128)(2,1)S(1)} %get-tuple-element.31.near_in, ...), custom_call_target="tpu_custom_call" | custom-call | flops 1006632960 | bytes 20971520 | tf_op jit(solution)/shard_map/terms/pallas_call | solution.py:95
  34.2 0.0 copy-done.3
  34.2 0.0 copy-done.4
  34.2 41.5 %exchange.5 = (f32[48,64,128]{2,1,0:T(8,128)S(1)}, f32[48,64,128]{2,1,0:T(8,128)S(1)}, bf16[48,64,128]{2,1,0:T(8,128)(2,1)S(1)}, bf16[48,64,128]{2,1,0:T(8,128)(2,1)S(1)}, bf16[48,64,128]{2,1,0:T(8,128)(2,1)S(1)}) custom-call(f32[48,64,128]{2,1,0:T(8,128)S(1)} %get-tuple-element.33.refs_0_, bf16[48,64,128]{2,1,0:T(8,128)(2,1)S(1)} %get-tuple-element.34.refs_1_, ...), custom_call_target="tpu_custom_call" | custom-call | tf_op jit(solution)/shard_map/exchange/pallas_call | solution.py:402
  75.7 10.7 %terms.4 = (f32[48,64,128]{2,1,0:T(8,128)S(1)}, bf16[48,64,128]{2,1,0:T(8,128)(2,1)S(1)}, f32[48,64,128]{2,1,0:T(8,128)S(1)}, f32[64,128]{1,0:T(8,128)}) custom-call(s32[192]{0:T(256)S(1)} %reshape.9.slots, bf16[48,64,128]{2,1,0:T(8,128)(2,1)S(1)} %get-tuple-element.36.far_in, bf16[48,64,128]{2,1,0:T(8,128)(2,1)S(1)} %get-tuple-element.37.near_in, ...), custom_call_target="tpu_custom_call" | custom-call | flops 1006632960 | bytes 20971520 | tf_op jit(solution)/shard_map/terms/pallas_call | solution.py:95
  86.4 46.8 %exchange.6 = (f32[48,64,128]{2,1,0:T(8,128)S(1)}, f32[48,64,128]{2,1,0:T(8,128)S(1)}, bf16[48,64,128]{2,1,0:T(8,128)(2,1)S(1)}, bf16[48,64,128]{2,1,0:T(8,128)(2,1)S(1)}, bf16[48,64,128]{2,1,0:T(8,128)(2,1)S(1)}) custom-call(f32[48,64,128]{2,1,0:T(8,128)S(1)} %get-tuple-element.40.refs_0_, bf16[48,64,128]{2,1,0:T(8,128)(2,1)S(1)} %get-tuple-element.41.refs_1_, ...), custom_call_target="tpu_custom_call" | custom-call | tf_op jit(solution)/shard_map/exchange/pallas_call | solution.py:402
  133.2 0.0 copy-start.1
  133.2 11.1 %terms.5 = (f32[48,64,128]{2,1,0:T(8,128)S(1)}, bf16[48,64,128]{2,1,0:T(8,128)(2,1)S(1)}, f32[48,64,128]{2,1,0:T(8,128)S(1)}, f32[64,128]{1,0:T(8,128)S(1)}, f32[48,64,128]{2,1,0:T(8,128)}) custom-call(s32[192]{0:T(256)S(1)} %reshape.9.slots, bf16[48,64,128]{2,1,0:T(8,128)(2,1)S(1)} %get-tuple-element.44.far_in, ...), custom_call_target="tpu_custom_call" | custom-call | flops 1006632960 | bytes 20971520 | tf_op jit(solution)/shard_map/terms/pallas_call | solution.py:95
  144.3 0.0 copy-done.1
  144.3 34.8 %exchange.7 = (f32[48,64,128]{2,1,0:T(8,128)S(1)}, f32[8,128]{1,0:T(8,128)S(1)}) custom-call(f32[48,64,128]{2,1,0:T(8,128)S(1)} %get-tuple-element.49.refs_0_, bf16[48,64,128]{2,1,0:T(8,128)(2,1)S(1)} %get-tuple-element.50.refs_1_, f32[48,64,128]{2,1,0:T(8,128)S(1)} %get-tuple-element.51.refs_2_, f32[48,64,128]{2,1,0:T(8,128)S(1)} %get-tuple-element.47.field.refs_3_, ...), custom_call_target="tpu_custom_call" | custom-call | tf_op jit(solution)/shard_map/exchange/pallas_call | solution.py:402
  179.1 0.5 slice_bitcast_fusion
  179.6 1.1 copy.11
  (1 shorter events, 0.0 us)
Async XLA Ops:
  1.5 1.4 copy-start
  2.9 20.8 %copy-start.2 = (bf16[48,128,128]{2,1,0:T(8,128)(2,1)S(1)}, bf16[48,128,128]{2,1,0:T(8,128)(2,1)}, u32[]{:S(2)}) copy-start(bf16[48,128,128]{2,1,0:T(8,128)(2,1)} %whiten.5) | copy-start | bytes 4718596
  23.8 10.4 %copy-start.3 = (s32[48,64,128]{2,1,0:T(8,128)S(1)}, s32[48,64,128]{2,1,0:T(8,128)}, u32[]{:S(2)}) copy-start(s32[48,64,128]{2,1,0:T(8,128)} %refs_5_.5) | copy-start | bytes 4718596
  23.8 10.4 %copy-start.4 = (f32[48,64,128]{2,1,0:T(8,128)S(1)}, f32[48,64,128]{2,1,0:T(8,128)}, u32[]{:S(2)}) copy-start(f32[48,64,128]{2,1,0:T(8,128)} %refs_7_.1) | copy-start | bytes 4718596
  133.2 11.1 %copy-start.1 = (f32[48,64,128]{2,1,0:T(8,128)S(1)}, f32[48,64,128]{2,1,0:T(8,128)}, u32[]{:S(2)}) copy-start(f32[48,64,128]{2,1,0:T(8,128)} %refs_6_.1) | copy-start | bytes 4718596

commit v4 on v3

--- a/solution.py
+++ b/solution.py
@@ -8,7 +8,7 @@
 from jax.sharding import PartitionSpec as P
 
 leap_size = 0.3
-GROUP = 8
+GROUP = 16
 PARTS = 6
 
 

time: 181 us -> 179 us (0.989)
  Pallas kernels: 176 us -> 174 us
    pallas_call x3, Pallas kernels: 32.1 us -> 29.8 us  [terms(): pl.pallas_call(functools.partial(terms_kernel, group), grid_spec=pltpu.Pr...]
where the time goes in v4:
time: 179 us; the launch traced here: 178 us
  Pallas kernels  174 us (97%)
  local copies, waits for them, and re-layouts  3.28 us (2%)
    pallas_call x4, Pallas kernels, exchange(): pl.pallas_call(functools.partial(exchange_kernel, count, parts, back, for...  144 us
    pallas_call x3, Pallas kernels, terms(): pl.pallas_call(functools.partial(terms_kernel, group), grid_spec=pltpu.Pr...  29.8 us

profile of v4, /device:TPU:0, one launch (start us, length us, event | category | flops | bytes accessed | tf_op | source)
XLA Modules:
  0.0 178.4 jit_solution(13036081392252589564)
XLA Ops:
  0.6 0.7 clamp_select_fusion
  1.3 0.1 copy.9
  1.4 0.1 reshape.9.slots
  1.5 0.0 copy-start
  1.5 1.4 copy-done
  2.9 0.0 copy-start.2
  2.9 20.8 %exchange.4 = (bf16[48,64,128]{2,1,0:T(8,128)(2,1)S(1)}, bf16[48,64,128]{2,1,0:T(8,128)(2,1)S(1)}, bf16[48,64,128]{2,1,0:T(8,128)(2,1)S(1)}) custom-call(f32[48,64,128]{2,1,0:T(8,128)S(1)} %copy-done), custom_call_target="tpu_custom_call" | custom-call | tf_op jit(solution)/shard_map/exchange/pallas_call | solution.py:402
  23.7 0.0 copy-done.2
  23.8 0.0 copy-start.3
  23.8 0.0 copy-start.4
  23.8 9.6 %terms.3 = (f32[48,64,128]{2,1,0:T(8,128)S(1)}, bf16[48,64,128]{2,1,0:T(8,128)(2,1)S(1)}, f32[48,64,128]{2,1,0:T(8,128)S(1)}, f32[64,128]{1,0:T(8,128)S(1)}) custom-call(s32[192]{0:T(256)S(1)} %reshape.9.slots, bf16[48,64,128]{2,1,0:T(8,128)(2,1)S(1)} %get-tuple-element.30.far_in, bf16[48,64,128]{2,1,0:T(8,128)(2,1)S(1)} %get-tuple-element.31.near_in, ...), custom_call_target="tpu_custom_call" | custom-call | flops 1006632960 | bytes 20971520 | tf_op jit(solution)/shard_map/terms/pallas_call | solution.py:95
  33.4 0.0 copy-done.3
  33.4 0.0 copy-done.4
  33.4 41.5 %exchange.5 = (f32[48,64,128]{2,1,0:T(8,128)S(1)}, f32[48,64,128]{2,1,0:T(8,128)S(1)}, bf16[48,64,128]{2,1,0:T(8,128)(2,1)S(1)}, bf16[48,64,128]{2,1,0:T(8,128)(2,1)S(1)}, bf16[48,64,128]{2,1,0:T(8,128)(2,1)S(1)}) custom-call(f32[48,64,128]{2,1,0:T(8,128)S(1)} %get-tuple-element.33.refs_0_, bf16[48,64,128]{2,1,0:T(8,128)(2,1)S(1)} %get-tuple-element.34.refs_1_, ...), custom_call_target="tpu_custom_call" | custom-call | tf_op jit(solution)/shard_map/exchange/pallas_call | solution.py:402
  74.9 9.9 %terms.4 = (f32[48,64,128]{2,1,0:T(8,128)S(1)}, bf16[48,64,128]{2,1,0:T(8,128)(2,1)S(1)}, f32[48,64,128]{2,1,0:T(8,128)S(1)}, f32[64,128]{1,0:T(8,128)}) custom-call(s32[192]{0:T(256)S(1)} %reshape.9.slots, bf16[48,64,128]{2,1,0:T(8,128)(2,1)S(1)} %get-tuple-element.36.far_in, bf16[48,64,128]{2,1,0:T(8,128)(2,1)S(1)} %get-tuple-element.37.near_in, ...), custom_call_target="tpu_custom_call" | custom-call | flops 1006632960 | bytes 20971520 | tf_op jit(solution)/shard_map/terms/pallas_call | solution.py:95
  84.8 46.8 %exchange.6 = (f32[48,64,128]{2,1,0:T(8,128)S(1)}, f32[48,64,128]{2,1,0:T(8,128)S(1)}, bf16[48,64,128]{2,1,0:T(8,128)(2,1)S(1)}, bf16[48,64,128]{2,1,0:T(8,128)(2,1)S(1)}, bf16[48,64,128]{2,1,0:T(8,128)(2,1)S(1)}) custom-call(f32[48,64,128]{2,1,0:T(8,128)S(1)} %get-tuple-element.40.refs_0_, bf16[48,64,128]{2,1,0:T(8,128)(2,1)S(1)} %get-tuple-element.41.refs_1_, ...), custom_call_target="tpu_custom_call" | custom-call | tf_op jit(solution)/shard_map/exchange/pallas_call | solution.py:402
  131.6 0.0 copy-start.1
  131.7 10.3 %terms.5 = (f32[48,64,128]{2,1,0:T(8,128)S(1)}, bf16[48,64,128]{2,1,0:T(8,128)(2,1)S(1)}, f32[48,64,128]{2,1,0:T(8,128)S(1)}, f32[64,128]{1,0:T(8,128)S(1)}, f32[48,64,128]{2,1,0:T(8,128)}) custom-call(s32[192]{0:T(256)S(1)} %reshape.9.slots, bf16[48,64,128]{2,1,0:T(8,128)(2,1)S(1)} %get-tuple-element.44.far_in, ...), custom_call_target="tpu_custom_call" | custom-call | flops 1006632960 | bytes 20971520 | tf_op jit(solution)/shard_map/terms/pallas_call | solution.py:95
  141.9 0.0 copy-done.1
  141.9 34.8 %exchange.7 = (f32[48,64,128]{2,1,0:T(8,128)S(1)}, f32[8,128]{1,0:T(8,128)S(1)}) custom-call(f32[48,64,128]{2,1,0:T(8,128)S(1)} %get-tuple-element.49.refs_0_, bf16[48,64,128]{2,1,0:T(8,128)(2,1)S(1)} %get-tuple-element.50.refs_1_, f32[48,64,128]{2,1,0:T(8,128)S(1)} %get-tuple-element.51.refs_2_, f32[48,64,128]{2,1,0:T(8,128)S(1)} %get-tuple-element.47.field.refs_3_, ...), custom_call_target="tpu_custom_call" | custom-call | tf_op jit(solution)/shard_map/exchange/pallas_call | solution.py:402
  176.8 0.5 slice_bitcast_fusion
  177.3 1.1 copy.11
  (1 shorter events, 0.0 us)
Async XLA Ops:
  1.5 1.4 copy-start
  2.9 20.8 %copy-start.2 = (bf16[48,128,128]{2,1,0:T(8,128)(2,1)S(1)}, bf16[48,128,128]{2,1,0:T(8,128)(2,1)}, u32[]{:S(2)}) copy-start(bf16[48,128,128]{2,1,0:T(8,128)(2,1)} %whiten.5) | copy-start | bytes 4718596
  23.8 9.7 %copy-start.3 = (s32[48,64,128]{2,1,0:T(8,128)S(1)}, s32[48,64,128]{2,1,0:T(8,128)}, u32[]{:S(2)}) copy-start(s32[48,64,128]{2,1,0:T(8,128)} %refs_5_.5) | copy-start | bytes 4718596
  23.8 9.7 %copy-start.4 = (f32[48,64,128]{2,1,0:T(8,128)S(1)}, f32[48,64,128]{2,1,0:T(8,128)}, u32[]{:S(2)}) copy-start(f32[48,64,128]{2,1,0:T(8,128)} %refs_7_.1) | copy-start | bytes 4718596
  131.6 10.3 %copy-start.1 = (f32[48,64,128]{2,1,0:T(8,128)S(1)}, f32[48,64,128]{2,1,0:T(8,128)}, u32[]{:S(2)}) copy-start(f32[48,64,128]{2,1,0:T(8,128)} %refs_6_.1) | copy-start | bytes 4718596

commit v5 on v4

--- a/solution.py
+++ b/solution.py
@@ -168,6 +168,8 @@
 
     def load(at, c):
         source, target = loads[at]
+        if at:
+            return pltpu.make_async_copy(source, target, load_sem.at[at, 0])
         return pltpu.make_async_copy(source.at[cut[c]], target.at[cut[c]], load_sem.at[at, c])
 
     if back:
@@ -176,9 +178,8 @@
             loads += [(start_hbm, start), (push_hbm, push)]
     else:
         loads = [(field_hbm, field)]
-    for at in range(len(loads)):
-        for c in range(parts):
-            load(at, c).start()
+    for c in range(parts):
+        load(0, c).start()
 
     barrier = pltpu.get_barrier_semaphore()
     pl.semaphore_signal(barrier, inc=1, device_id={"blk": pair}, device_id_type=pl.DeviceIdType.MESH)
@@ -236,6 +237,8 @@
     if back:
         for c in range(parts):
             swap(c).start()
+        for at in range(1, len(loads)):
+            load(at, 0).start()
 
         @pl.when(jnp.logical_not(has_next))
         def _():
@@ -257,8 +260,11 @@
     if energy:
         gain[...] = 0.5 * square[...]
     for c in range(parts):
-        for at in range(1 if back else 0, len(loads)):
-            load(at, c).wait()
+        if not back:
+            load(0, c).wait()
+        elif c == 0:
+            for at in range(1, len(loads)):
+                load(at, 0).wait()
         if back:
             @pl.when(has_next)
             def _():

time: 179 us -> 178 us (level)
  no operation moved by 1% of the time
where the time goes in v5:
time: 178 us
  Pallas kernels  173 us (97%)
  local copies, waits for them, and re-layouts  3.28 us (2%)
    pallas_call x4, Pallas kernels, exchange(): pl.pallas_call(functools.partial(exchange_kernel, count, parts, back, for...  143 us
    pallas_call x3, Pallas kernels, terms(): pl.pallas_call(functools.partial(terms_kernel, group), grid_spec=pltpu.Pr...  29.9 us

profile of v5, /device:TPU:0, one launch (start us, length us, event | category | flops | bytes accessed | tf_op | source)
XLA Modules:
  0.0 177.6 jit_solution(3160302805828580394)
XLA Ops:
  0.6 0.7 clamp_select_fusion
  1.3 0.1 copy.9
  1.4 0.1 reshape.9.slots
  1.5 0.0 copy-start
  1.5 1.4 copy-done
  2.9 0.0 copy-start.2
  2.9 20.8 %exchange.4 = (bf16[48,64,128]{2,1,0:T(8,128)(2,1)S(1)}, bf16[48,64,128]{2,1,0:T(8,128)(2,1)S(1)}, bf16[48,64,128]{2,1,0:T(8,128)(2,1)S(1)}) custom-call(f32[48,64,128]{2,1,0:T(8,128)S(1)} %copy-done), custom_call_target="tpu_custom_call" | custom-call | tf_op jit(solution)/shard_map/exchange/pallas_call | solution.py:408
  23.7 0.0 copy-done.2
  23.8 0.0 copy-start.3
  23.8 0.0 copy-start.4
  23.8 9.7 %terms.3 = (f32[48,64,128]{2,1,0:T(8,128)S(1)}, bf16[48,64,128]{2,1,0:T(8,128)(2,1)S(1)}, f32[48,64,128]{2,1,0:T(8,128)S(1)}, f32[64,128]{1,0:T(8,128)S(1)}) custom-call(s32[192]{0:T(256)S(1)} %reshape.9.slots, bf16[48,64,128]{2,1,0:T(8,128)(2,1)S(1)} %get-tuple-element.30.far_in, bf16[48,64,128]{2,1,0:T(8,128)(2,1)S(1)} %get-tuple-element.31.near_in, ...), custom_call_target="tpu_custom_call" | custom-call | flops 1006632960 | bytes 20971520 | tf_op jit(solution)/shard_map/terms/pallas_call | solution.py:95
  33.4 0.0 copy-done.3
  33.4 0.0 copy-done.4
  33.5 41.1 %exchange.5 = (f32[48,64,128]{2,1,0:T(8,128)S(1)}, f32[48,64,128]{2,1,0:T(8,128)S(1)}, bf16[48,64,128]{2,1,0:T(8,128)(2,1)S(1)}, bf16[48,64,128]{2,1,0:T(8,128)(2,1)S(1)}, bf16[48,64,128]{2,1,0:T(8,128)(2,1)S(1)}) custom-call(f32[48,64,128]{2,1,0:T(8,128)S(1)} %get-tuple-element.33.refs_0_, bf16[48,64,128]{2,1,0:T(8,128)(2,1)S(1)} %get-tuple-element.34.refs_1_, ...), custom_call_target="tpu_custom_call" | custom-call | tf_op jit(solution)/shard_map/exchange/pallas_call | solution.py:408
  74.5 10.0 %terms.4 = (f32[48,64,128]{2,1,0:T(8,128)S(1)}, bf16[48,64,128]{2,1,0:T(8,128)(2,1)S(1)}, f32[48,64,128]{2,1,0:T(8,128)S(1)}, f32[64,128]{1,0:T(8,128)}) custom-call(s32[192]{0:T(256)S(1)} %reshape.9.slots, bf16[48,64,128]{2,1,0:T(8,128)(2,1)S(1)} %get-tuple-element.36.far_in, bf16[48,64,128]{2,1,0:T(8,128)(2,1)S(1)} %get-tuple-element.37.near_in, ...), custom_call_target="tpu_custom_call" | custom-call | flops 1006632960 | bytes 20971520 | tf_op jit(solution)/shard_map/terms/pallas_call | solution.py:95
  84.5 46.8 %exchange.6 = (f32[48,64,128]{2,1,0:T(8,128)S(1)}, f32[48,64,128]{2,1,0:T(8,128)S(1)}, bf16[48,64,128]{2,1,0:T(8,128)(2,1)S(1)}, bf16[48,64,128]{2,1,0:T(8,128)(2,1)S(1)}, bf16[48,64,128]{2,1,0:T(8,128)(2,1)S(1)}) custom-call(f32[48,64,128]{2,1,0:T(8,128)S(1)} %get-tuple-element.40.refs_0_, bf16[48,64,128]{2,1,0:T(8,128)(2,1)S(1)} %get-tuple-element.41.refs_1_, ...), custom_call_target="tpu_custom_call" | custom-call | tf_op jit(solution)/shard_map/exchange/pallas_call | solution.py:408
  131.4 0.0 copy-start.1
  131.4 10.3 %terms.5 = (f32[48,64,128]{2,1,0:T(8,128)S(1)}, bf16[48,64,128]{2,1,0:T(8,128)(2,1)S(1)}, f32[48,64,128]{2,1,0:T(8,128)S(1)}, f32[64,128]{1,0:T(8,128)S(1)}, f32[48,64,128]{2,1,0:T(8,128)}) custom-call(s32[192]{0:T(256)S(1)} %reshape.9.slots, bf16[48,64,128]{2,1,0:T(8,128)(2,1)S(1)} %get-tuple-element.44.far_in, ...), custom_call_target="tpu_custom_call" | custom-call | flops 1006632960 | bytes 20971520 | tf_op jit(solution)/shard_map/terms/pallas_call | solution.py:95
  141.7 0.0 copy-done.1
  141.7 34.3 %exchange.7 = (f32[48,64,128]{2,1,0:T(8,128)S(1)}, f32[8,128]{1,0:T(8,128)S(1)}) custom-call(f32[48,64,128]{2,1,0:T(8,128)S(1)} %get-tuple-element.49.refs_0_, bf16[48,64,128]{2,1,0:T(8,128)(2,1)S(1)} %get-tuple-element.50.refs_1_, f32[48,64,128]{2,1,0:T(8,128)S(1)} %get-tuple-element.51.refs_2_, f32[48,64,128]{2,1,0:T(8,128)S(1)} %get-tuple-element.47.field.refs_3_, ...), custom_call_target="tpu_custom_call" | custom-call | tf_op jit(solution)/shard_map/exchange/pallas_call | solution.py:408
  176.0 0.5 slice_bitcast_fusion
  176.5 1.1 copy.11
  (1 shorter events, 0.0 us)
Async XLA Ops:
  1.5 1.4 copy-start
  2.9 20.8 %copy-start.2 = (bf16[48,128,128]{2,1,0:T(8,128)(2,1)S(1)}, bf16[48,128,128]{2,1,0:T(8,128)(2,1)}, u32[]{:S(2)}) copy-start(bf16[48,128,128]{2,1,0:T(8,128)(2,1)} %whiten.5) | copy-start | bytes 4718596
  23.8 9.7 %copy-start.3 = (s32[48,64,128]{2,1,0:T(8,128)S(1)}, s32[48,64,128]{2,1,0:T(8,128)}, u32[]{:S(2)}) copy-start(s32[48,64,128]{2,1,0:T(8,128)} %refs_5_.5) | copy-start | bytes 4718596
  23.8 9.7 %copy-start.4 = (f32[48,64,128]{2,1,0:T(8,128)S(1)}, f32[48,64,128]{2,1,0:T(8,128)}, u32[]{:S(2)}) copy-start(f32[48,64,128]{2,1,0:T(8,128)} %refs_7_.1) | copy-start | bytes 4718596
  131.4 10.3 %copy-start.1 = (f32[48,64,128]{2,1,0:T(8,128)S(1)}, f32[48,64,128]{2,1,0:T(8,128)}, u32[]{:S(2)}) copy-start(f32[48,64,128]{2,1,0:T(8,128)} %refs_6_.1) | copy-start | bytes 4718596
